TPU v7x, 512 devices: a whole 4x4x16 slice. The times are simulated.
512 devices in a mesh: dp: 16 (over y, z_hi, core), ctx: 32 (over x, z_lo).
Axes of the slice: x: 4, y: 4, z: 16 (z_hi: 2, z_lo: 8; z = z_hi * 8 + z_lo), core: 2. Of those that a mesh axis runs over, the one named last changes fastest.
Arguments:
- query_act: bfloat16 [16, 4096, 4096], P('dp', 'ctx'), may hold values from -6 to 6
- gated_input: bfloat16 [16, 4096, 4096], P('dp', 'ctx'), may hold values from -6 to 6
- out_grad: bfloat16 [16, 4096, 4096], P('dp', 'ctx'), may hold values from -6 to 6
- filter_taps: float32 [4096, 4096], P('dp', 'ctx'), may hold values from -0.09375 to 0.09375
Outputs:
- input_grad: bfloat16 [16, 4096, 4096], P('dp', 'ctx')
- taps_grad: float32 [4096, 4096], P('dp', 'ctx')
All inputs are finite; a program needn't handle non-finite values.
Results may differ from a plain program's by a relative error of at most 0.0049.
Values may be sent and summed in bfloat16 or wider, within the bound.
No kernel may reach another device: no remote copies, remote signals or barrier semaphores. Data moves between devices by JAX's collectives and lax.ppermute only.
A program may use at most 128 MiB of HBM per device.

v0:
```python
import math

import jax
import jax.numpy as jnp
from jax import lax
from jax.sharding import PartitionSpec as P

inner_width = 64
highest = lax.Precision.HIGHEST


def outer_table(outer_size, half_rows, sign):
    total_size = outer_size * inner_width
    shape = (inner_width, outer_size, half_rows)
    inner_index = lax.broadcasted_iota(jnp.int32, shape, 0)
    freq_index = lax.broadcasted_iota(jnp.int32, shape, 1)
    row_index = lax.broadcasted_iota(jnp.int32, shape, 2)
    angle = (freq_index * (row_index * inner_width + inner_index) % total_size).astype(
        jnp.float32
    ) * (2.0 * math.pi / total_size)
    cosine = jnp.cos(angle)
    sine = jnp.sin(angle) * sign
    real_row = jnp.stack([cosine, -sine], 2)
    imag_row = jnp.stack([sine, cosine], 2)
    return jnp.stack([real_row, imag_row], 1)


def inner_table(sign):
    row_index = lax.broadcasted_iota(jnp.int32, (inner_width, inner_width), 0)
    col_index = lax.broadcasted_iota(jnp.int32, (inner_width, inner_width), 1)
    angle = (row_index * col_index % inner_width).astype(jnp.float32) * (
        2.0 * math.pi / inner_width
    )
    cosine = jnp.cos(angle)
    sine = jnp.sin(angle) * sign
    real_row = jnp.stack([cosine, -sine], 1)
    imag_row = jnp.stack([sine, cosine], 1)
    return jnp.stack([real_row, imag_row], 0)


def forward_real(section_table, signal):
    first = jnp.einsum("bpkn,nbc->pkbc", section_table[:, :, :, 0], signal, precision=highest)
    return jnp.einsum("pjqa,qkac->pkjc", inner_table(-1.0), first, precision=highest)


def forward_complex(section_table, signal):
    first = jnp.einsum("bpkqn,qnbc->pkbc", section_table, signal, precision=highest)
    return jnp.einsum("pjqa,qkac->pkjc", inner_table(-1.0), first, precision=highest)


def inverse_complex(spectrum):
    outer_size = spectrum.shape[1]
    half_rows = outer_size // 2
    total_size = outer_size * inner_width
    first = jnp.einsum("pjqa,qkac->pkjc", inner_table(1.0), spectrum, precision=highest)
    back_table = jnp.transpose(outer_table(outer_size, half_rows, 1.0), (0, 1, 4, 3, 2))
    result = jnp.einsum("bpnqk,qkbc->pnbc", back_table, first, precision=highest)
    return result / total_size


def mirrored(spectrum):
    reversed_rows = jnp.roll(jnp.flip(spectrum, 1), 1, 1)
    columns = jnp.flip(reversed_rows, 2)
    top_row = jnp.roll(columns[:, :1], 1, 2)
    return jnp.concatenate([top_row, columns[:, 1:]], 1)


def body(query_act, gated_input, out_grad, filter_taps):
    product = (out_grad.astype(jnp.float32) * query_act.astype(jnp.float32)).astype(jnp.bfloat16)
    stacked = jnp.stack([product, gated_input], 0)
    moved = lax.all_to_all(stacked, "ctx", split_axis=3, concat_axis=2, tiled=True)
    length = moved.shape[2]
    channels = moved.shape[3]
    half_rows = length // inner_width
    outer_size = 2 * half_rows
    section_table = outer_table(outer_size, half_rows, -1.0)
    packed = forward_complex(
        section_table, moved.reshape(2, half_rows, inner_width, channels).astype(jnp.float32)
    )
    share_taps = lax.all_to_all(filter_taps, "dp", split_axis=1, concat_axis=0, tiled=True)
    share_spec = forward_real(
        section_table, share_taps.reshape(half_rows, inner_width, share_taps.shape[1])
    )
    taps_spec = lax.all_gather(share_spec, "dp", axis=3, tiled=True)
    mirror = mirrored(packed)
    prod_real = 0.5 * (packed[0] + mirror[0])
    prod_imag = 0.5 * (packed[1] - mirror[1])
    gated_real = 0.5 * (packed[1] + mirror[1])
    gated_imag = 0.5 * (mirror[0] - packed[0])
    first_real = prod_real * taps_spec[0] + prod_imag * taps_spec[1]
    first_imag = prod_imag * taps_spec[0] - prod_real * taps_spec[1]
    second_real = prod_real * gated_real + prod_imag * gated_imag
    second_imag = prod_imag * gated_real - prod_real * gated_imag
    combined = jnp.stack([first_real - second_imag, first_imag + second_real], 0)
    result = inverse_complex(combined)
    grad_rows = result[0].reshape(length, channels).astype(jnp.bfloat16)
    cross_rows = result[1].reshape(length, channels)
    input_grad = lax.all_to_all(grad_rows[None], "ctx", split_axis=1, concat_axis=2, tiled=True)
    normalizer = 1.0 / math.sqrt(length * lax.axis_size("dp"))
    taps_share_sum = lax.psum_scatter(cross_rows, "dp", scatter_dimension=0, tiled=True)
    return (input_grad, taps_share_sum * normalizer)


def solution(mesh):
    in_specs = (P("dp", "ctx", None), P("dp", "ctx", None), P("dp", "ctx", None), P("dp", "ctx"))
    out_specs = (P("dp", "ctx", None), P("dp", "ctx"))
    return jax.shard_map(body, mesh=mesh, in_specs=in_specs, out_specs=out_specs, check_vma=False)
```

profile of v0, /device:TPU:6, one launch (start us, length us, event | category | flops | bytes accessed | tf_op | source)
XLA Modules:
  0.0 578.7 jit_solution(12045599816694453038)
XLA Ops:
  7.2 1.7 copy.59
  8.8 17.8 %all-to-all-start.1 = ((f32[256,16,8]{0,2,1:T(8,128)}), f32[256,16,8]{0,2,1:T(8,128)S(1)}, u32[]{:S(2)}, u32[]{:S(2)}) async-start(f32[256,16,8]{0,2,1:T(8,128)} %bitcast.21), calls=%async_computation.1 | async-start | bytes 262144 | tf_op jit(solution)/shard_map/all_to_all | solution.py:80
  27.2 8.5 %fusion.35 = (f32[64,128,1,64]{1,3,2,0:T(8,128)S(1)}, f32[64,128,1,64]{1,3,2,0:T(8,128)S(1)}, f32[64,128,1,64]{1,3,2,0:T(8,128)S(1)}, f32[64,128,1,64]{1,3,2,0:T(8,128)S(1)}, f32[64,128,1,64]{1,3,2,0:T(8,128)S(1)}) fusion(s32[64]{0:T(128)S(1)} %iota_multiply_fusion), kind=kLoop, calls=%fused_computation.53 | loop fusion | flops 9437184 | bytes 10486016 | tf_op jit(solution)/shard_map/neg | solution.py:23
  35.7 6.6 %fusion.12 = (f32[64,1,128,2,64]{2,4,3,1,0:T(8,128)}, f32[64,1,128,2,64]{2,4,3,0,1:T(8,128)}, f32[64,1,128,2,64]{2,4,3,0,1:T(8,128)}, f32[64,1,128,2,64]{2,4,3,1,0:T(8,128)}) fusion(f32[64,128,1,64]{1,3,2,0:T(8,128)S(1)} %get-tuple-element.24, f32[64,128,1,64]{1,3,2,0:T(8,128)S(1)} %get-tuple-element.20, f32[64,128,1,64]{1,3,2,0:T(8,128)S(1)} %get-tuple-element.23, ...), kind=kLoop, calls=%fused_computation.19 | loop fusion | flops 4194304 | bytes 27262976 | tf_op jit(solution)/shard_map/stack | solution.py:25
  42.7 4.1 fusion.32
  46.8 1.6 convolution_bitcast_fusion.1
  48.9 3.8 copy.53
  52.7 215.0 %all_to_all.49 = bf16[2,1,128,4096]{2,0,1,3:T(2,128)(2,1)S(1)} all-to-all(bf16[2,1,128,4096]{2,0,1,3:T(2,128)(2,1)} %copy.53), channel_id=1, replica_groups=mesh['dp'=16,'ctx'=32] {'ctx'}, dimensions={3} | all-to-all | bytes 4194304 | tf_op jit(solution)/shard_map/all_to_all | solution.py:71
  267.7 1.7 copy.54
  269.4 3.1 copy.55
  272.5 12.0 %fusion.18 = f32[2,128,64,128,1]{1,3,0,2,4:T(8,128)} fusion(f32[64,1,128,2,64]{2,4,3,1,0:T(8,128)} %get-tuple-element.15, f32[64,1,128,2,64]{2,4,3,1,0:T(8,128)} %get-tuple-element.12, bf16[2,64,64,128,1]{3,2,1,0,4:T(8,128)(2,1)S(1)} %bitcast.102), kind=kOutput, calls=%fused_computation.33 | convolution fusion | flops 3223322624 | bytes 18874368 | tf_op jit(solution)/shard_map/bpkqn,qnbc->pkbc/dot_general | solution.py:47
  284.5 8.8 %copy.74 = f32[2,128,64,128,1]{3,2,0,4,1:T(8,128)} copy(f32[2,128,64,128,1]{1,3,0,2,4:T(8,128)} %fusion.18) | data formatting | bytes 16777216 | tf_op jit(solution)/shard_map/bpkqn,qnbc->pkbc/transpose | solution.py:47
  293.3 10.7 %convolution_bitcast_fusion = f32[2,128,64,128]{3,2,0,1:T(8,128)S(1)} fusion(f32[2,128,64,128,1]{3,2,0,4,1:T(8,128)} %copy.74, f32[1,64,2,64]{3,1,2,0:T(8,128)S(1)} %get-tuple-element.18, f32[1,64,2,64]{3,1,2,0:T(8,128)S(1)} %get-tuple-element.19), kind=kOutput, calls=%fused_computation.35 | convolution fusion | flops 3221241856 | bytes 16842752 | tf_op jit(solution)/shard_map/pjqa,qkac->pkjc/dot_general | solution.py:48
  304.1 4.7 slice.79
  309.8 11.9 %slice.67 = f32[2,127,64,128]{3,2,0,1:T(8,128)} reverse(f32[2,127,64,128]{3,2,0,1:T(8,128)} %slice.79), dimensions={1,2} | reverse | bytes 16646144 | tf_op jit(solution)/shard_map/slice | solution.py:65
  321.7 6.2 %pad_maximum_fusion = f32[2,128,64,128]{3,2,0,1:T(8,128)} fusion(f32[2,127,64,128]{3,2,0,1:T(8,128)} %slice.67, f32[2,1,63,128]{3,2,0,1:T(8,128)S(1)} %slice.65, f32[2,1,1,128]{3,2,0,1:T(1,128)S(1)} %slice.77), kind=kLoop, calls=%fused_computation.4 | loop fusion | flops 4194304 | bytes 16777216 | tf_op jit(solution)/shard_map/concatenate | solution.py:65
  327.9 8.4 %fusion.58 = (f32[1,128,64,128]{1,2,0,3:T(8,128)}, f32[1,128,64,128]{1,2,0,3:T(8,128)}) fusion(f32[2,128,64,128]{1,2,0,3:T(8,128)} %all-gather.2.cloned.1.call-done), kind=kLoop, calls=%fused_computation.88 | loop fusion | bytes 16777216 | tf_op jit(solution)/shard_map/slice | solution.py:90
  336.3 5.5 copy.95
  341.8 5.4 copy.94
  347.2 9.9 %subtract_subtract_fusion = (f32[1,128,64,128]{3,2,0,1:T(8,128)S(1)}, f32[1,128,64,128]{3,2,0,1:T(8,128)S(1)}) fusion(f32[1,128,64,128]{3,2,0,1:T(8,128)} %copy.95, f32[1,128,64,128]{3,2,0,1:T(8,128)} %copy.94, f32[2,128,64,128]{3,2,0,1:T(8,128)} %pad_maximum_fusion, f32[2,128,64,128]{3,2,0,1:T(8,128)} %copy-done), kind=kLoop, calls=%fused_computation.28 | loop fusion | flops 23068672 | bytes 33554432 | tf_op jit(solution)/shard_map/sub | solution.py:94
  357.1 8.8 %fusion.21 = f32[2,128,64,128,1]{3,2,0,1,4:T(8,128)S(1)} fusion(f32[1,128,64,128]{3,2,0,1:T(8,128)S(1)} %get-tuple-element.9, f32[1,128,64,128]{3,2,0,1:T(8,128)S(1)} %get-tuple-element.8, f32[1,64,2,64]{3,1,2,0:T(8,128)S(1)} %get-tuple-element.17, f32[1,64,2,64]{3,1,2,0:T(8,128)S(1)} %get-tuple-element.16), kind=kOutput, calls=%fused_computation.34 | convolution fusion | flops 3223339008 | bytes 16842752 | tf_op jit(solution)/shard_map/pjqa,qkac->pkjc/dot_general | solution.py:55
  365.9 20.3 %fusion.17 = f32[2,64,64,128]{3,1,0,2:T(8,128)} fusion(f32[2,128,64,128,1]{3,2,0,1,4:T(8,128)S(1)} %fusion.21, f32[64,1,128,2,64]{2,4,3,0,1:T(8,128)} %get-tuple-element.13, f32[64,1,128,2,64]{2,4,3,0,1:T(8,128)} %get-tuple-element.14), kind=kOutput, calls=%fused_computation.26 | convolution fusion | flops 3224371200 | bytes 20971520 | tf_op jit(solution)/shard_map/bpnqk,qkbc->pnbc/dot_general | solution.py:57
  386.2 1.8 slice.128
  388.7 16.7 %copy.109 = bf16[1,4096,128]{2,0,1:T(2,128)(2,1)S(1)} copy(bf16[1,4096,128]{2,1,0:T(8,128)(2,1)S(1)} %bitcast.107) | data formatting | bytes 2097152 | tf_op jit(solution)/shard_map/convert_element_type | solution.py:96
  406.0 22.6 %reduce = bf16[4096,128]{1,0:T(8,128)(2,1)S(1)} reduce(bf16[4096,1,128]{2,1,0:T(2,128)(2,1)S(1)} %bitcast.105, bf16[]{:T(256)} %broadcast.423), dimensions={1}, to_apply=%bitcast.101.reduce_sub_computation | reduce | bytes 2097154
  428.5 1.1 reshape.190
  429.7 9.2 %all-to-all-start.2 = ((bf16[32,2,8192]{2,1,0:T(2,128)(2,1)}), bf16[32,2,8192]{2,1,0:T(2,128)(2,1)S(1)}, u32[]{:S(2)}, u32[]{:S(2)}) async-start(bf16[32,2,8192]{2,1,0:T(2,128)(2,1)} %reshape.190), calls=%async_computation.2 | async-start | bytes 2097152 | tf_op jit(solution)/shard_map/all_to_all | solution.py:98
  438.9 2.6 copy.70
  441.5 125.4 %reduce-scatter.2.cloned.1.call-done = f32[256,128]{1,0:T(8,128)} async-done(((f32[4096,128]{1,0:T(8,128)}), f32[256,128]{1,0:T(8,128)}) %reduce-scatter.2.cloned.1.call-update) | async-done | bytes 131088 | tf_op jit(solution)/shard_map/reduce_scatter | solution.py:100
  566.9 1.6 broadcast_multiply_fusion.1
  568.5 1.0 reshape.191
  570.3 1.3 copy.71
  (34 shorter events, 4.3 us)
Async XLA Ops:
  8.8 33.5 %all-to-all-start.1 = ((f32[256,16,8]{0,2,1:T(8,128)}), f32[256,16,8]{0,2,1:T(8,128)S(1)}, u32[]{:S(2)}, u32[]{:S(2)}) async-start(f32[256,16,8]{0,2,1:T(8,128)} %bitcast.21), calls=%async_computation.1 | async-start | bytes 262144 | tf_op jit(solution)/shard_map/all_to_all | solution.py:80
  26.7 301.3 %all-gather.2.cloned.1.call-start = ((), (), s32[]{:S(2)}) async-start(), calls=%async_computation.4 | async-start | bytes 8912896 | tf_op jit(solution)/shard_map/all_gather | solution.py:84
  42.6 5.7 copy-start.1
  42.7 5.7 copy-start.2
  46.8 1.9 copy-start.3
  304.0 5.7 copy-start
  428.5 10.4 %slice-start = ((f32[2,64,64,128]{3,1,0,2:T(8,128)}), f32[1,64,64,128]{3,1,0,2:T(8,128)S(1)}, s32[]{:S(2)}) async-start(f32[2,64,64,128]{3,1,0,2:T(8,128)} %fusion.17), calls=%async_computation.6 | async-start | bytes 4194304 | tf_op jit(solution)/shard_map/slice | solution.py:97
  429.7 138.8 %all-to-all-start.2 = ((bf16[32,2,8192]{2,1,0:T(2,128)(2,1)}), bf16[32,2,8192]{2,1,0:T(2,128)(2,1)S(1)}, u32[]{:S(2)}, u32[]{:S(2)}) async-start(bf16[32,2,8192]{2,1,0:T(2,128)(2,1)} %reshape.190), calls=%async_computation.2 | async-start | bytes 2097152 | tf_op jit(solution)/shard_map/all_to_all | solution.py:98
  438.9 128.0 %reduce-scatter.2.cloned.1.call-start = ((), (), s32[]{:S(2)}) async-start(), calls=%async_computation.5 | async-start | bytes 2228224 | tf_op jit(solution)/shard_map/reduce_scatter | solution.py:100
Sparse Core Ops, SparseCore 0:
  48.5 178.6 all-gather.1
  444.5 122.3 reduce-scatter.1
where the time goes:
time: 586 us; the launch traced here: 579 us
  blocking collectives  215 us (37%)
  waiting for transfers between devices  125 us (21%)
  local copies, waits for them, and re-layouts  82.8 us (14%)
  matrix products  57.5 us (10%)
  other arithmetic  56.3 us (10%)
  starting transfers between devices  27.1 us (5%)
  between operations  14.5 us (2%)
    all_to_all x1, blocking collectives, body(): lax.all_to_all(stacked, 'ctx', split_axis=3, concat_axis=2, tiled=True)  215 us
    reduce_scatter x1, waiting for transfers between devices, body(): lax.psum_scatter(cross_rows, 'dp', scatter_dimension=0, tiled=True)  125 us
    unnamed x1, other arithmetic  22.6 us
    dot_general x1, matrix products, inverse_complex(): jnp.einsum('bpnqk,qkbc->pnbc', back_table, first, precision=highest)  20.3 us
    all_to_all x1, starting transfers between devices, body(): lax.all_to_all(filter_taps, 'dp', split_axis=1, concat_axis=0, tiled=True)  17.8 us
    unnamed x16, local copies, waits for them, and re-layouts  17.7 us
    convert_element_type x1, local copies, waits for them, and re-layouts, body(): grad_rows = result[0].reshape(length, channels).astype(jnp.bfloat16)  16.7 us
    dot_general x1, matrix products, forward_complex(): jnp.einsum('bpkqn,qnbc->pkbc', section_table, signal, precision=highest)  12 us
  transfers between devices with their start and end apart: 4, of which 1 were waited for; matrix products, arithmetic and copies ran while one was open for 14% of the time, Pallas kernels for 0%

commit v1 on v0

v1 whole, which is shorter than its diff:
```python
import functools
import math

import jax
import jax.numpy as jnp
import ml_dtypes
import numpy as np
from jax import lax
from jax.experimental import pallas as pl
from jax.experimental.pallas import tpu as pltpu
from jax.sharding import PartitionSpec as P

bf16 = jnp.bfloat16
f32 = jnp.float32
fine = 128
coarse = 32
group = 8
groups = fine // group
vmem_limit = 56 * 1024 * 1024


def split_table(table):
    high = table.astype(ml_dtypes.bfloat16)
    low = (table - high.astype(np.float64)).astype(ml_dtypes.bfloat16)
    return np.stack([high, low], 0)


@functools.lru_cache(maxsize=None)
def make_tables():
    k0 = np.arange(coarse)[:, None, None]
    q = np.arange(coarse)[None, :, None]
    j = np.arange(fine)[None, None, :]
    angle = 2.0 * np.pi * (((2 * k0 + 1) * (fine * q + j)) % 16384) / 16384.0
    parts = np.stack([np.cos(angle), -np.sin(angle)], 1)
    parts = parts.reshape(coarse, 2, coarse, groups, group)
    full = np.zeros((groups, coarse, 2, group, coarse, group))
    for lane in range(group):
        full[:, :, :, lane, :, lane] = np.transpose(parts[..., lane], (3, 0, 1, 2))
    full = full.reshape(groups, coarse * 2 * group, coarse * group)
    back = np.transpose(full, (0, 2, 1)) * (2.0 / 8192.0)
    angle = 2.0 * np.pi * (np.outer(np.arange(fine), np.arange(fine)) % fine) / fine
    cosine, sine = np.cos(angle), np.sin(angle)
    inner = np.block([[cosine, sine], [-sine, cosine]])
    return split_table(full), split_table(back), split_table(inner), split_table(inner.T)


def dot(a, b):
    return jnp.dot(a, b, preferred_element_type=f32)


def split(value):
    high = value.astype(bf16)
    return high, (value - high.astype(f32)).astype(bf16)


def dot3(table_high, table_low, value):
    high, low = split(value)
    return dot(table_high, high) + (dot(table_low, high) + dot(table_high, low))


def coarse_forward(x_ref, wide_ref, table_ref, mid_ref):
    def widen(q, carry):
        wide_ref[q] = x_ref[q].astype(f32)
        return carry

    lax.fori_loop(0, coarse, widen, 0, unroll=4)

    def step(g, carry):
        rows = pl.ds(pl.multiple_of(g * group, group), group)
        value = wide_ref[:, rows, :].reshape(coarse * group, fine).astype(bf16)
        result = dot(table_ref[0, g], value) + dot(table_ref[1, g], value)
        mid_ref[:, rows, :] = result.reshape(2 * coarse, group, fine)
        return carry

    lax.fori_loop(0, groups, step, 0, unroll=2)


def coarse_backward(mid_ref, back_ref, out_ref):
    def step(g, carry):
        rows = pl.ds(pl.multiple_of(g * group, group), group)
        value = mid_ref[:, rows, :].reshape(2 * coarse * group, fine)
        result = dot3(back_ref[0, g], back_ref[1, g], value)
        out_ref[:, rows, :] = result.reshape(coarse, group, fine)
        return carry

    lax.fori_loop(0, groups, step, 0, unroll=2)


def fine_forward(mid_ref, inner_ref, k):
    value = mid_ref[pl.ds(2 * k, 2)].reshape(2 * fine, fine)
    return dot3(inner_ref[0], inner_ref[1], value)


def times_conj(a, b):
    a_re, a_im, b_re, b_im = a[:fine], a[fine:], b[:fine], b[fine:]
    return jnp.concatenate([a_re * b_re + a_im * b_im, a_im * b_re - a_re * b_im], 0)


def spectrum_kernel(x_ref, table_ref, inner_ref, spec_ref, wide_ref, mid_ref):
    coarse_forward(x_ref, wide_ref, table_ref, mid_ref)

    def step(k, carry):
        spec_ref[k] = fine_forward(mid_ref, inner_ref, k)
        return carry

    lax.fori_loop(0, coarse, step, 0, unroll=2)


def grad_kernel(x_ref, taps_ref, table_ref, back_ref, inner_ref, outer_ref, y_ref, spec_ref, wide_ref, mid_ref):
    coarse_forward(x_ref, wide_ref, table_ref, mid_ref)

    def step(k, carry):
        spec = fine_forward(mid_ref, inner_ref, k)
        spec_ref[k] = spec
        result = dot3(outer_ref[0], outer_ref[1], times_conj(spec, taps_ref[k]))
        mid_ref[pl.ds(2 * k, 2)] = result.reshape(2, fine, fine)
        return carry

    lax.fori_loop(0, coarse, step, 0, unroll=2)
    coarse_backward(mid_ref, back_ref, wide_ref)

    def narrow(q, carry):
        y_ref[q] = wide_ref[q].astype(bf16)
        return carry

    lax.fori_loop(0, coarse, narrow, 0, unroll=4)


def cross_kernel(x_ref, prod_ref, table_ref, back_ref, inner_ref, outer_ref, y_ref, wide_ref, mid_ref):
    coarse_forward(x_ref, wide_ref, table_ref, mid_ref)

    def step(k, carry):
        spec = fine_forward(mid_ref, inner_ref, k)
        result = dot3(outer_ref[0], outer_ref[1], times_conj(prod_ref[k], spec))
        mid_ref[pl.ds(2 * k, 2)] = result.reshape(2, fine, fine)
        return carry

    lax.fori_loop(0, coarse, step, 0, unroll=2)
    coarse_backward(mid_ref, back_ref, y_ref)


scratch = [pltpu.VMEM((coarse, fine, fine), f32), pltpu.VMEM((2 * coarse, fine, fine), f32)]
spec_shape = jax.ShapeDtypeStruct((coarse, 2 * fine, fine), f32)
params = pltpu.CompilerParams(vmem_limit_bytes=vmem_limit)


def call(kernel, out_shape, flops, *args):
    in_bytes = sum(a.size * a.dtype.itemsize for a in args)
    return pl.pallas_call(
        kernel,
        out_shape=out_shape,
        scratch_shapes=scratch,
        compiler_params=params,
        cost_estimate=pl.CostEstimate(flops=flops, bytes_accessed=in_bytes, transcendentals=0),
    )(*args)


def product_kernel(grad_ref, query_ref, out_ref):
    value = (grad_ref[0].astype(f32) * query_ref[0].astype(f32)).astype(bf16)
    for i in range(out_ref.shape[0]):
        out_ref[i] = value[:, i * fine : (i + 1) * fine]


def block_kernel(value_ref, out_ref):
    for i in range(out_ref.shape[0]):
        out_ref[i] = value_ref[0, :, i * fine : (i + 1) * fine]


def unblock_kernel(value_ref, out_ref):
    for i in range(value_ref.shape[0]):
        out_ref[0, :, i * fine : (i + 1) * fine] = value_ref[i]


blocks_a_step = 8


def to_blocks(kernel, *args):
    wide = pl.BlockSpec((1, fine, blocks_a_step * fine), lambda i: (0, 0, i))
    return pl.pallas_call(
        kernel,
        grid=(coarse // blocks_a_step,),
        in_specs=[wide] * len(args),
        out_specs=pl.BlockSpec((blocks_a_step, fine, fine), lambda i: (i, 0, 0)),
        out_shape=jax.ShapeDtypeStruct((coarse, fine, fine), bf16),
        compiler_params=params,
    )(*args)


def from_blocks(value):
    return pl.pallas_call(
        unblock_kernel,
        grid=(coarse // blocks_a_step,),
        in_specs=[pl.BlockSpec((blocks_a_step, fine, fine), lambda i: (i, 0, 0))],
        out_specs=pl.BlockSpec((1, fine, blocks_a_step * fine), lambda i: (0, 0, i)),
        out_shape=jax.ShapeDtypeStruct((1, fine, coarse * fine), bf16),
        compiler_params=params,
    )(value)


def to_owners(blocks):
    return lax.all_to_all(blocks, "ctx", 0, 0, tiled=True)


def swap(value, bit):
    return lax.ppermute(value, "dp", [(i, i ^ bit) for i in range(16)])


def turn(value, by):
    return lax.ppermute(value, "dp", [(i, (i + 4 * by) % 16) for i in range(16)])


def place():
    index = lax.axis_index("dp")
    return index // 4, index // 2 % 2, index % 2


def pair(mine, other, bit):
    return jnp.where(bit == 0, jnp.stack([mine, other]), jnp.stack([other, mine]))


def gather_taps(taps):
    y, z_hi, core = place()
    both = pair(taps, swap(taps, 2), z_hi)
    both = pair(both, swap(both, 1), core)
    both = jnp.transpose(both, (1, 0, 2, 3))
    whole = jnp.zeros((4,) + both.shape, both.dtype)
    whole = lax.dynamic_update_index_in_dim(whole, both, y, 0)
    for by in (1, 3, 2):
        whole = lax.dynamic_update_index_in_dim(whole, turn(both, by), (y - by) % 4, 0)
    return whole.reshape(coarse, fine, fine)


def sum_over_dp(cross):
    y, z_hi, core = place()
    parts = cross.reshape(4, 2, 2, 256, fine)
    away = lax.dynamic_index_in_dim(parts, 1 - core, 2, keepdims=False)
    kept = lax.dynamic_index_in_dim(parts, core, 2, keepdims=False) + swap(away, 1)
    total = lax.dynamic_index_in_dim(kept, y, 0, keepdims=False)
    for by in (1, 3, 2):
        away = lax.dynamic_index_in_dim(kept, (y + by) % 4, 0, keepdims=False)
        total = total + turn(away.astype(bf16), by).astype(f32)
    away = lax.dynamic_index_in_dim(total, 1 - z_hi, 0, keepdims=False)
    return lax.dynamic_index_in_dim(total, z_hi, 0, keepdims=False) + swap(away.astype(bf16), 2).astype(f32)


def body(query_act, gated_input, out_grad, filter_taps):
    table, back, inner, outer = (jnp.asarray(t) for t in make_tables())
    product = to_owners(to_blocks(product_kernel, out_grad, query_act))
    gated = to_owners(to_blocks(block_kernel, gated_input))
    taps = gather_taps(filter_taps.astype(bf16))
    one = 2 * 256 * 256 * 256 * 32
    taps_spec = call(spectrum_kernel, spec_shape, 3 * one, taps, table, inner)
    grad_rows, prod_spec = call(
        grad_kernel,
        (jax.ShapeDtypeStruct((coarse, fine, fine), bf16), spec_shape),
        6 * one,
        product, taps_spec, table, back, inner, outer,
    )
    input_grad = from_blocks(to_owners(grad_rows))
    cross = call(
        cross_kernel,
        jax.ShapeDtypeStruct((coarse, fine, fine), f32),
        6 * one,
        gated, prod_spec, table, back, inner, outer,
    )
    return input_grad, sum_over_dp(cross) * (1.0 / 256.0)


def solution(mesh):
    in_specs = (P("dp", "ctx", None), P("dp", "ctx", None), P("dp", "ctx", None), P("dp", "ctx"))
    out_specs = (P("dp", "ctx", None), P("dp", "ctx"))
    return jax.shard_map(body, mesh=mesh, in_specs=in_specs, out_specs=out_specs, check_vma=False)
```

time: 586 us -> 289 us (0.49)
  the two profiles are of different devices: /device:TPU:6 before, /device:TPU:195 now
where the time goes in v1:
time: 289 us; the launch traced here: 288 us
  starting transfers between devices  116 us (40%)
  Pallas kernels  90.4 us (31%)
  waiting for transfers between devices  75.1 us (26%)
  local copies, waits for them, and re-layouts  3.71 us (1%)
    pallas_call x3, Pallas kernels, call(): pl.pallas_call(kernel, out_shape=out_shape, scratch_shapes=scratch, compi...  79.9 us
    all_to_all x3, starting transfers between devices, to_owners(): return lax.all_to_all(blocks, 'ctx', 0, 0, tiled=True)  70.7 us
    all_to_all x3, waiting for transfers between devices, to_owners(): return lax.all_to_all(blocks, 'ctx', 0, 0, tiled=True)  42.3 us
    ppermute x4, starting transfers between devices, swap(): return lax.ppermute(value, 'dp', [(i, i ^ bit) for i in range(16)])  24.7 us
    ppermute x4, waiting for transfers between devices, swap(): return lax.ppermute(value, 'dp', [(i, i ^ bit) for i in range(16)])  21.7 us
    ppermute x6, starting transfers between devices, turn(): lax.ppermute(value, 'dp', [(i, (i + 4 * by) % 16) for i in range(16)])  20.5 us
    ppermute x6, waiting for transfers between devices, turn(): lax.ppermute(value, 'dp', [(i, (i + 4 * by) % 16) for i in range(16)])  11.2 us
    pallas_call x2, Pallas kernels, to_blocks(): pl.pallas_call(kernel, grid=(coarse // blocks_a_step,), in_specs=[wide] *...  7.09 us
  transfers between devices with their start and end apart: 13, of which 10 were waited for; matrix products, arithmetic and copies ran while one was open for 1% of the time, Pallas kernels for 29%

profile of v1, /device:TPU:195, one launch (start us, length us, event | category | flops | bytes accessed | tf_op | source)
XLA Modules:
  0.0 288.4 jit_solution(14383281950817396411)
XLA Ops:
  0.6 3.7 %shard_map.95 = bf16[32,128,128]{2,1,0:T(8,128)(2,1)} custom-call(bf16[1,128,4096]{2,1,0:T(8,128)(2,1)} %grad_ref.1, bf16[1,128,4096]{2,1,0:T(8,128)(2,1)} %query_ref.1), custom_call_target="tpu_custom_call" | custom-call | tf_op jit(solution)/shard_map/pallas_call | solution.py:179
  4.3 12.4 %all-to-all-start = ((bf16[32,128,128]{2,1,0:T(8,128)(2,1)}), bf16[32,128,128]{2,1,0:T(8,128)(2,1)S(1)}, u32[]{:S(2)}, u32[]{:S(2)}) async-start(bf16[32,128,128]{2,1,0:T(8,128)(2,1)} %shard_map.95), calls=%async_computation | async-start | bytes 2097152 | tf_op jit(solution)/shard_map/all_to_all | solution.py:201
  16.7 3.4 %shard_map.99 = bf16[32,128,128]{2,1,0:T(8,128)(2,1)} custom-call(bf16[1,128,4096]{2,1,0:T(8,128)(2,1)} %value_ref.1), custom_call_target="tpu_custom_call" | custom-call | tf_op jit(solution)/shard_map/pallas_call | solution.py:179
  20.1 42.3 %all-to-all-done.x_ref = bf16[32,128,128]{2,1,0:T(8,128)(2,1)S(1)} async-done(((bf16[32,128,128]{2,1,0:T(8,128)(2,1)}), bf16[32,128,128]{2,1,0:T(8,128)(2,1)S(1)}, u32[]{:S(2)}, u32[]{:S(2)}) %all-to-all-start) | async-done | bytes 1048608 | tf_op jit(solution)/shard_map/all_to_all | solution.py:201
  62.4 11.0 %all-to-all-start.2 = ((bf16[32,128,128]{2,1,0:T(8,128)(2,1)}), bf16[32,128,128]{2,1,0:T(8,128)(2,1)S(1)}, u32[]{:S(2)}, u32[]{:S(2)}) async-start(bf16[32,128,128]{2,1,0:T(8,128)(2,1)} %shard_map.99), calls=%async_computation.2 | async-start | bytes 2097152 | tf_op jit(solution)/shard_map/all_to_all | solution.py:201
  73.5 7.9 %collective-permute-start = (bf16[256,128]{1,0:T(8,128)(2,1)S(1)}, bf16[256,128]{1,0:T(8,128)(2,1)S(1)}, u32[]{:S(2)}, u32[]{:S(2)}) collective-permute-start(bf16[256,128]{1,0:T(8,128)(2,1)S(1)} %convert_element_type.39), channel_id=1, source_target_pairs={{0,64},{32,96},{64,0},{96,32},{128,192},{160,224},{192,128},{224,1... | collective-permute-start | bytes 196616 | tf_op jit(solution)/shard_map/ppermute | solution.py:205
  81.5 5.8 %collective-permute-done = bf16[256,128]{1,0:T(8,128)(2,1)S(1)} collective-permute-done((bf16[256,128]{1,0:T(8,128)(2,1)S(1)}, bf16[256,128]{1,0:T(8,128)(2,1)S(1)}, u32[]{:S(2)}, u32[]{:S(2)}) %collective-permute-start) | collective-permute-done | bytes 65568 | tf_op jit(solution)/shard_map/ppermute | solution.py:205
  87.3 6.5 %collective-permute-start.1 = (bf16[2,256,128]{2,1,0:T(8,128)(2,1)S(1)}, bf16[2,256,128]{2,1,0:T(8,128)(2,1)S(1)}, u32[]{:S(2)}, u32[]{:S(2)}) collective-permute-start(bf16[2,256,128]{2,1,0:T(8,128)(2,1)S(1)} %maximum_select_fusion.2), channel_id=1, source_target_pairs={{0,32},{32,0},{64,96},{96,64},{128,160},{160,128},{192,224},{224,1... | collective-permute-start | bytes 393224 | tf_op jit(solution)/shard_map/ppermute | solution.py:205
  93.9 0.9 collective-permute-done.1
  94.8 3.2 %collective-permute-start.2 = (bf16[2,2,256,128]{3,2,0,1:T(8,128)(2,1)S(1)}, bf16[2,2,256,128]{3,2,0,1:T(8,128)(2,1)S(1)}, u32[]{:S(2)}, u32[]{:S(2)}) collective-permute-start(bf16[2,2,256,128]{3,2,0,1:T(8,128)(2,1)S(1)} %get-tuple-element.9), channel_id=1, source_target_pairs={{0,128},{32,160},{64,192},{96,224},{128,256},{160,288},{192,320},{... | collective-permute-start | bytes 786440 | tf_op jit(solution)/shard_map/ppermute | solution.py:209
  98.1 3.4 %collective-permute-start.3 = (bf16[2,2,256,128]{3,2,0,1:T(8,128)(2,1)S(1)}, bf16[2,2,256,128]{3,2,0,1:T(8,128)(2,1)S(1)}, u32[]{:S(2)}, u32[]{:S(2)}) collective-permute-start(bf16[2,2,256,128]{3,2,0,1:T(8,128)(2,1)S(1)} %get-tuple-element.9), channel_id=1, source_target_pairs={{0,384},{32,416},{64,448},{96,480},{128,0},{160,32},{192,64},{224,... | collective-permute-start | bytes 786440 | tf_op jit(solution)/shard_map/ppermute | solution.py:209
  101.5 3.5 %collective-permute-start.4 = (bf16[2,2,256,128]{3,2,0,1:T(8,128)(2,1)S(1)}, bf16[2,2,256,128]{3,2,0,1:T(8,128)(2,1)S(1)}, u32[]{:S(2)}, u32[]{:S(2)}) collective-permute-start(bf16[2,2,256,128]{3,2,0,1:T(8,128)(2,1)S(1)} %get-tuple-element.9), channel_id=1, source_target_pairs={{0,256},{32,288},{64,320},{96,352},{128,384},{160,416},{192,448},{... | collective-permute-start | bytes 786440 | tf_op jit(solution)/shard_map/ppermute | solution.py:209
  105.6 1.6 collective-permute-done.3
  107.2 4.6 %collective-permute-done.4 = bf16[2,2,256,128]{3,2,0,1:T(8,128)(2,1)S(1)} collective-permute-done((bf16[2,2,256,128]{3,2,0,1:T(8,128)(2,1)S(1)}, bf16[2,2,256,128]{3,2,0,1:T(8,128)(2,1)S(1)}, u32[]{:S(2)}, u32[]{:S(2)}) %collective-permute-start.4) | collective-permute-done | bytes 262176 | tf_op jit(solution)/shard_map/ppermute | solution.py:209
  111.9 1.0 copy-done.2
  112.9 15.3 %shard_map.96.taps_ref = f32[32,256,128]{2,1,0:T(8,128)} custom-call(bf16[32,128,128]{2,1,0:T(8,128)(2,1)} %bitcast.47, bf16[2,16,512,256]{3,2,1,0:T(8,128)(2,1)} %constant.134.clone.table_ref, bf16[2,256,256]{2,1,0:T(8,128)(2,1)} %constant.136.clone.inner_ref), custom_call_target="tpu_custom_call" | custom-call | flops 3221225472 | bytes 9699328 | tf_op jit(solution)/shard_map/pallas_call | solution.py:149
  128.2 32.8 %shard_map.97 = (bf16[32,128,128]{2,1,0:T(8,128)(2,1)}, f32[32,256,128]{2,1,0:T(8,128)}) custom-call(bf16[32,128,128]{2,1,0:T(8,128)(2,1)} %copy-done.4, f32[32,256,128]{2,1,0:T(8,128)} %shard_map.96.taps_ref, bf16[2,16,512,256]{3,2,1,0:T(8,128)(2,1)} %constant.134.clone.table_ref, bf16[2,16,256,512]{3,2,1,0:T(8,128)(2,1)} %constant.135.clone.back_ref, ...), custom_call_target="tpu_custom_call" | custom-call | flops 6442450944 | bytes 22544384 | tf_op jit(solution)/shard_map/pallas_call | solution.py:149
  161.0 47.3 %all-to-all-start.1 = ((bf16[32,128,128]{2,1,0:T(8,128)(2,1)}), bf16[32,128,128]{2,1,0:T(8,128)(2,1)S(1)}, u32[]{:S(2)}, u32[]{:S(2)}) async-start(bf16[32,128,128]{2,1,0:T(8,128)(2,1)} %get-tuple-element.4), calls=%async_computation.1 | async-start | bytes 2097152 | tf_op jit(solution)/shard_map/all_to_all | solution.py:201
  208.3 31.7 %shard_map.100 = f32[32,128,128]{2,1,0:T(8,128)} custom-call(bf16[32,128,128]{2,1,0:T(8,128)(2,1)} %copy-done, f32[32,256,128]{2,1,0:T(8,128)} %get-tuple-element.5.prod_ref, bf16[2,16,512,256]{3,2,1,0:T(8,128)(2,1)} %constant.134.clone.table_ref, bf16[2,16,256,512]{3,2,1,0:T(8,128)(2,1)} %constant.135.clone.back_ref, ...), custom_call_target="tpu_custom_call" | custom-call | flops 6442450944 | bytes 22544384 | tf_op jit(solution)/shard_map/pallas_call | solution.py:149
  240.0 1.3 dynamic-slice_bitcast_fusion
  241.3 4.2 %collective-permute-start.5 = (f32[4,2,256,128]{3,2,1,0:T(8,128)S(1)}, f32[4,2,256,128]{3,2,1,0:T(8,128)S(1)}, u32[]{:S(2)}, u32[]{:S(2)}) collective-permute-start(f32[4,2,256,128]{3,2,1,0:T(8,128)S(1)} %dynamic-slice_bitcast_fusion), channel_id=1, source_target_pairs={{0,32},{32,0},{64,96},{96,64},{128,160},{160,128},{192,224},{224,1... | collective-permute-start | bytes 3145736 | tf_op jit(solution)/shard_map/ppermute | solution.py:205
  245.6 2.2 collective-permute-done.5
  247.8 1.3 bitcast_add_fusion
  249.2 4.7 %collective-permute-start.6 = (bf16[2,256,128]{2,1,0:T(8,128)(2,1)S(1)}, bf16[2,256,128]{2,1,0:T(8,128)(2,1)S(1)}, u32[]{:S(2)}, u32[]{:S(2)}) collective-permute-start(bf16[2,256,128]{2,1,0:T(8,128)(2,1)S(1)} %get-tuple-element.6), channel_id=1, source_target_pairs={{0,128},{32,160},{64,192},{96,224},{128,256},{160,288},{192,320},{... | collective-permute-start | bytes 393224 | tf_op jit(solution)/shard_map/ppermute | solution.py:209
  253.9 2.6 collective-permute-start.7
  256.6 3.1 %collective-permute-start.8 = (bf16[2,256,128]{2,1,0:T(8,128)(2,1)S(1)}, bf16[2,256,128]{2,1,0:T(8,128)(2,1)S(1)}, u32[]{:S(2)}, u32[]{:S(2)}) collective-permute-start(bf16[2,256,128]{2,1,0:T(8,128)(2,1)S(1)} %get-tuple-element.7), channel_id=1, source_target_pairs={{0,256},{32,288},{64,320},{96,352},{128,384},{160,416},{192,448},{... | collective-permute-start | bytes 393224 | tf_op jit(solution)/shard_map/ppermute | solution.py:209
  260.2 4.1 %collective-permute-done.8 = bf16[2,256,128]{2,1,0:T(8,128)(2,1)S(1)} collective-permute-done((bf16[2,256,128]{2,1,0:T(8,128)(2,1)S(1)}, bf16[2,256,128]{2,1,0:T(8,128)(2,1)S(1)}, u32[]{:S(2)}, u32[]{:S(2)}) %collective-permute-start.8) | collective-permute-done | bytes 131104 | tf_op jit(solution)/shard_map/ppermute | solution.py:209
  264.4 6.1 %collective-permute-start.9 = (bf16[256,128]{1,0:T(8,128)(2,1)S(1)}, bf16[256,128]{1,0:T(8,128)(2,1)S(1)}, u32[]{:S(2)}, u32[]{:S(2)}) collective-permute-start(bf16[256,128]{1,0:T(8,128)(2,1)S(1)} %fusion.6), channel_id=1, source_target_pairs={{0,64},{32,96},{64,0},{96,32},{128,192},{160,224},{192,128},{224,1... | collective-permute-start | bytes 196616 | tf_op jit(solution)/shard_map/ppermute | solution.py:205
  270.5 12.8 %collective-permute-done.9 = bf16[256,128]{1,0:T(8,128)(2,1)S(1)} collective-permute-done((bf16[256,128]{1,0:T(8,128)(2,1)S(1)}, bf16[256,128]{1,0:T(8,128)(2,1)S(1)}, u32[]{:S(2)}, u32[]{:S(2)}) %collective-permute-start.9) | collective-permute-done | bytes 65568 | tf_op jit(solution)/shard_map/ppermute | solution.py:205
  283.2 0.7 fusion.5
  283.9 1.0 copy-done.1
  284.9 3.5 %shard_map.98 = bf16[1,128,4096]{2,1,0:T(8,128)(2,1)} custom-call(bf16[32,128,128]{2,1,0:T(8,128)(2,1)} %copy-done.1), custom_call_target="tpu_custom_call" | custom-call | tf_op jit(solution)/shard_map/pallas_call | solution.py:190
  (27 shorter events, 1.4 us)
Async XLA Ops:
  0.6 72.8 %copy-start.3 = (f32[256,128]{1,0:T(8,128)S(1)}, f32[256,128]{1,0:T(8,128)}, u32[]{:S(2)}) copy-start(f32[256,128]{1,0:T(8,128)} %param.11) | copy-start | bytes 393220
  4.3 58.1 %all-to-all-start = ((bf16[32,128,128]{2,1,0:T(8,128)(2,1)}), bf16[32,128,128]{2,1,0:T(8,128)(2,1)S(1)}, u32[]{:S(2)}, u32[]{:S(2)}) async-start(bf16[32,128,128]{2,1,0:T(8,128)(2,1)} %shard_map.95), calls=%async_computation | async-start | bytes 2097152 | tf_op jit(solution)/shard_map/all_to_all | solution.py:201
  62.4 65.8 %copy-start.4 = (bf16[32,128,128]{2,1,0:T(8,128)(2,1)}, bf16[32,128,128]{2,1,0:T(8,128)(2,1)S(1)}, u32[]{:S(2)}) copy-start(bf16[32,128,128]{2,1,0:T(8,128)(2,1)S(1)} %all-to-all-done.x_ref) | copy-start | bytes 3145732
  62.4 98.6 %all-to-all-start.2 = ((bf16[32,128,128]{2,1,0:T(8,128)(2,1)}), bf16[32,128,128]{2,1,0:T(8,128)(2,1)S(1)}, u32[]{:S(2)}, u32[]{:S(2)}) async-start(bf16[32,128,128]{2,1,0:T(8,128)(2,1)} %shard_map.99), calls=%async_computation.2 | async-start | bytes 2097152 | tf_op jit(solution)/shard_map/all_to_all | solution.py:201
  73.5 13.8 %collective-permute-start = (bf16[256,128]{1,0:T(8,128)(2,1)S(1)}, bf16[256,128]{1,0:T(8,128)(2,1)S(1)}, u32[]{:S(2)}, u32[]{:S(2)}) collective-permute-start(bf16[256,128]{1,0:T(8,128)(2,1)S(1)} %convert_element_type.39), channel_id=1, source_target_pairs={{0,64},{32,96},{64,0},{96,32},{128,192},{160,224},{192,128},{224,1... | collective-permute-start | bytes 196616 | tf_op jit(solution)/shard_map/ppermute | solution.py:205
  87.3 7.5 %collective-permute-start.1 = (bf16[2,256,128]{2,1,0:T(8,128)(2,1)S(1)}, bf16[2,256,128]{2,1,0:T(8,128)(2,1)S(1)}, u32[]{:S(2)}, u32[]{:S(2)}) collective-permute-start(bf16[2,256,128]{2,1,0:T(8,128)(2,1)S(1)} %maximum_select_fusion.2), channel_id=1, source_target_pairs={{0,32},{32,0},{64,96},{96,64},{128,160},{160,128},{192,224},{224,1... | collective-permute-start | bytes 393224 | tf_op jit(solution)/shard_map/ppermute | solution.py:205
  94.8 10.8 %collective-permute-start.2 = (bf16[2,2,256,128]{3,2,0,1:T(8,128)(2,1)S(1)}, bf16[2,2,256,128]{3,2,0,1:T(8,128)(2,1)S(1)}, u32[]{:S(2)}, u32[]{:S(2)}) collective-permute-start(bf16[2,2,256,128]{3,2,0,1:T(8,128)(2,1)S(1)} %get-tuple-element.9), channel_id=1, source_target_pairs={{0,128},{32,160},{64,192},{96,224},{128,256},{160,288},{192,320},{... | collective-permute-start | bytes 786440 | tf_op jit(solution)/shard_map/ppermute | solution.py:209
  98.1 9.1 %collective-permute-start.3 = (bf16[2,2,256,128]{3,2,0,1:T(8,128)(2,1)S(1)}, bf16[2,2,256,128]{3,2,0,1:T(8,128)(2,1)S(1)}, u32[]{:S(2)}, u32[]{:S(2)}) collective-permute-start(bf16[2,2,256,128]{3,2,0,1:T(8,128)(2,1)S(1)} %get-tuple-element.9), channel_id=1, source_target_pairs={{0,384},{32,416},{64,448},{96,480},{128,0},{160,32},{192,64},{224,... | collective-permute-start | bytes 786440 | tf_op jit(solution)/shard_map/ppermute | solution.py:209
  101.5 10.4 %collective-permute-start.4 = (bf16[2,2,256,128]{3,2,0,1:T(8,128)(2,1)S(1)}, bf16[2,2,256,128]{3,2,0,1:T(8,128)(2,1)S(1)}, u32[]{:S(2)}, u32[]{:S(2)}) collective-permute-start(bf16[2,2,256,128]{3,2,0,1:T(8,128)(2,1)S(1)} %get-tuple-element.9), channel_id=1, source_target_pairs={{0,256},{32,288},{64,320},{96,352},{128,384},{160,416},{192,448},{... | collective-permute-start | bytes 786440 | tf_op jit(solution)/shard_map/ppermute | solution.py:209
  111.9 1.0 copy-start.2
  161.0 47.3 %copy-start = (bf16[32,128,128]{2,1,0:T(8,128)(2,1)}, bf16[32,128,128]{2,1,0:T(8,128)(2,1)S(1)}, u32[]{:S(2)}) copy-start(bf16[32,128,128]{2,1,0:T(8,128)(2,1)S(1)} %all-to-all-done.2.x_ref) | copy-start | bytes 3145732
  161.0 122.9 %all-to-all-start.1 = ((bf16[32,128,128]{2,1,0:T(8,128)(2,1)}), bf16[32,128,128]{2,1,0:T(8,128)(2,1)S(1)}, u32[]{:S(2)}, u32[]{:S(2)}) async-start(bf16[32,128,128]{2,1,0:T(8,128)(2,1)} %get-tuple-element.4), calls=%async_computation.1 | async-start | bytes 2097152 | tf_op jit(solution)/shard_map/all_to_all | solution.py:201
  241.3 6.5 %collective-permute-start.5 = (f32[4,2,256,128]{3,2,1,0:T(8,128)S(1)}, f32[4,2,256,128]{3,2,1,0:T(8,128)S(1)}, u32[]{:S(2)}, u32[]{:S(2)}) collective-permute-start(f32[4,2,256,128]{3,2,1,0:T(8,128)S(1)} %dynamic-slice_bitcast_fusion), channel_id=1, source_target_pairs={{0,32},{32,0},{64,96},{96,64},{128,160},{160,128},{192,224},{224,1... | collective-permute-start | bytes 3145736 | tf_op jit(solution)/shard_map/ppermute | solution.py:205
  249.2 10.4 %collective-permute-start.6 = (bf16[2,256,128]{2,1,0:T(8,128)(2,1)S(1)}, bf16[2,256,128]{2,1,0:T(8,128)(2,1)S(1)}, u32[]{:S(2)}, u32[]{:S(2)}) collective-permute-start(bf16[2,256,128]{2,1,0:T(8,128)(2,1)S(1)} %get-tuple-element.6), channel_id=1, source_target_pairs={{0,128},{32,160},{64,192},{96,224},{128,256},{160,288},{192,320},{... | collective-permute-start | bytes 393224 | tf_op jit(solution)/shard_map/ppermute | solution.py:209
  253.9 6.3 %collective-permute-start.7 = (bf16[2,256,128]{2,1,0:T(8,128)(2,1)S(1)}, bf16[2,256,128]{2,1,0:T(8,128)(2,1)S(1)}, u32[]{:S(2)}, u32[]{:S(2)}) collective-permute-start(bf16[2,256,128]{2,1,0:T(8,128)(2,1)S(1)} %get-tuple-element.8), channel_id=1, source_target_pairs={{0,384},{32,416},{64,448},{96,480},{128,0},{160,32},{192,64},{224,... | collective-permute-start | bytes 393224 | tf_op jit(solution)/shard_map/ppermute | solution.py:209
  256.6 7.8 %collective-permute-start.8 = (bf16[2,256,128]{2,1,0:T(8,128)(2,1)S(1)}, bf16[2,256,128]{2,1,0:T(8,128)(2,1)S(1)}, u32[]{:S(2)}, u32[]{:S(2)}) collective-permute-start(bf16[2,256,128]{2,1,0:T(8,128)(2,1)S(1)} %get-tuple-element.7), channel_id=1, source_target_pairs={{0,256},{32,288},{64,320},{96,352},{128,384},{160,416},{192,448},{... | collective-permute-start | bytes 393224 | tf_op jit(solution)/shard_map/ppermute | solution.py:209
  264.4 18.8 %collective-permute-start.9 = (bf16[256,128]{1,0:T(8,128)(2,1)S(1)}, bf16[256,128]{1,0:T(8,128)(2,1)S(1)}, u32[]{:S(2)}, u32[]{:S(2)}) collective-permute-start(bf16[256,128]{1,0:T(8,128)(2,1)S(1)} %fusion.6), channel_id=1, source_target_pairs={{0,64},{32,96},{64,0},{96,32},{128,192},{160,224},{192,128},{224,1... | collective-permute-start | bytes 196616 | tf_op jit(solution)/shard_map/ppermute | solution.py:205
  283.9 1.0 copy-start.1

commit v2 on v1

v2 whole, which is shorter than its diff:
```python
import functools
import math

import jax
import jax.numpy as jnp
import ml_dtypes
import numpy as np
from jax import lax
from jax.experimental import pallas as pl
from jax.experimental.pallas import tpu as pltpu
from jax.sharding import PartitionSpec as P

bf16 = jnp.bfloat16
f32 = jnp.float32
fine = 128
coarse = 32
group = 8
groups = fine // group
unrolled = 8
vmem_limit = 56 * 1024 * 1024


def split_table(table):
    high = table.astype(ml_dtypes.bfloat16)
    low = (table - high.astype(np.float64)).astype(ml_dtypes.bfloat16)
    return np.concatenate([high, low, high], 1)


@functools.lru_cache(maxsize=None)
def make_tables():
    k0, q, j = np.arange(coarse), np.arange(coarse), np.arange(fine)
    angle = 2.0 * np.pi * (np.outer(2 * k0 + 1, q) % 128) / 128.0
    parts = np.stack([np.cos(angle), -np.sin(angle)], 1).reshape(2 * coarse, coarse)
    forward = np.kron(parts, np.eye(group))
    backward = forward.T * (2.0 / 8192.0)
    angle = 2.0 * np.pi * np.outer(2 * k0 + 1, j) / 16384.0
    twiddle = np.stack([np.cos(angle), np.sin(angle)], 1).astype(np.float32)
    twiddle = np.ascontiguousarray(np.broadcast_to(twiddle[..., None], twiddle.shape + (fine,)))
    angle = 2.0 * np.pi * (np.outer(j, j) % fine) / fine
    cosine, sine = np.cos(angle), np.sin(angle)
    inner = np.block([[cosine, sine], [-sine, cosine]])
    return split_table(forward), split_table(backward), twiddle, split_table(inner), split_table(inner.T)


def dot(a, b):
    return jnp.dot(a, b, preferred_element_type=f32)


def split_dot(table_ref, value):
    high = value.astype(bf16)
    low = (value - high.astype(f32)).astype(bf16)
    return dot(table_ref[...], jnp.concatenate([high, high, low], 0))


def copy(source, target, sem):
    return pltpu.make_async_copy(source, target, sem)


def coarse_forward(x_ref, forward_ref, mid_ref):
    depth = coarse * group

    def step(g, carry):
        rows = pl.ds(pl.multiple_of(g * 2 * group, 2 * group), 2 * group)
        value = x_ref[:, rows, :].astype(f32)
        value = [value[:, i * group : (i + 1) * group, :].reshape(depth, fine) for i in (0, 1)]
        value = jnp.concatenate(value, 1).astype(bf16)
        result = dot(forward_ref[:, :depth], value) + dot(forward_ref[:, depth : 2 * depth], value)
        result = [result[:, i * fine : (i + 1) * fine].reshape(2 * coarse, group, fine) for i in (0, 1)]
        mid_ref[:, rows, :] = jnp.concatenate(result, 1)
        return carry

    lax.fori_loop(0, groups // 2, step, 0, unroll=unrolled)


def coarse_backward(mid_ref, backward_ref, out_ref, out, sems):
    def sent(g):
        rows = pl.ds(pl.multiple_of(g * 2 * group, 2 * group), 2 * group)
        return rows, copy(out_ref.at[:, rows, :], out.at[:, rows, :], sems.at[g])

    def step(g, carry):
        rows, leaving = sent(g)
        value = mid_ref[:, rows, :]
        value = [value[:, i * group : (i + 1) * group, :].reshape(2 * coarse * group, fine) for i in (0, 1)]
        result = split_dot(backward_ref, jnp.concatenate(value, 1))
        result = [result[:, i * fine : (i + 1) * fine].reshape(coarse, group, fine) for i in (0, 1)]
        out_ref[:, rows, :] = jnp.concatenate(result, 1).astype(out_ref.dtype)
        leaving.start()
        return carry

    lax.fori_loop(0, groups // 2, step, 0, unroll=unrolled)

    def finish(g, carry):
        sent(g)[1].wait()
        return carry

    lax.fori_loop(0, groups // 2, finish, 0)


def fine_forward(mid_ref, twiddle_ref, inner_ref, k):
    turned = []
    for i in (0, 1):
        re, im = mid_ref[4 * k + 2 * i], mid_ref[4 * k + 2 * i + 1]
        cosine, sine = twiddle_ref[2 * k + i, 0], twiddle_ref[2 * k + i, 1]
        turned.append(jnp.concatenate([re * cosine + im * sine, im * cosine - re * sine], 0))
    return split_dot(inner_ref, jnp.concatenate(turned, 1))


def fine_backward(mid_ref, twiddle_ref, outer_ref, k, spec):
    result = split_dot(outer_ref, spec)
    for i in (0, 1):
        columns = slice(i * fine, (i + 1) * fine)
        re, im = result[:fine, columns], result[fine:, columns]
        cosine, sine = twiddle_ref[2 * k + i, 0], twiddle_ref[2 * k + i, 1]
        mid_ref[4 * k + 2 * i] = re * cosine - im * sine
        mid_ref[4 * k + 2 * i + 1] = re * sine + im * cosine


def times_conj(a, b):
    a_re, a_im, b_re, b_im = a[:fine], a[fine:], b[:fine], b[fine:]
    return jnp.concatenate([a_re * b_re + a_im * b_im, a_im * b_re - a_re * b_im], 0)


def load(hbm, vmem, sems):
    copies = [copy(h, v, sems.at[i]) for i, (h, v) in enumerate(zip(hbm, vmem))]
    for c in copies:
        c.start()
    return copies


def spectrum_kernel(x, forward, inner, twiddle, spec, *scratch):
    vmem, (spec_ref, mid_ref, sems, out_sems) = scratch[:4], scratch[4:]
    x_ref, forward_ref, inner_ref, twiddle_ref = vmem
    copies = load((x, forward, inner, twiddle), vmem, sems)
    copies[0].wait()
    copies[1].wait()
    coarse_forward(x_ref, forward_ref, mid_ref)
    copies[2].wait()
    copies[3].wait()

    def step(k, carry):
        spec_ref[k] = fine_forward(mid_ref, twiddle_ref, inner_ref, k)
        copy(spec_ref.at[k], spec.at[k], out_sems.at[k]).start()
        return carry

    lax.fori_loop(0, coarse // 2, step, 0, unroll=unrolled)

    def finish(k, carry):
        copy(spec_ref.at[k], spec.at[k], out_sems.at[k]).wait()
        return carry

    lax.fori_loop(0, coarse // 2, finish, 0)


def grad_kernel(x, forward, inner, twiddle, taps, outer, backward, y, spec, *scratch):
    vmem, (y_ref, spec_ref, mid_ref, sems, out_sems) = scratch[:7], scratch[7:]
    x_ref, forward_ref, inner_ref, twiddle_ref, taps_ref, outer_ref, backward_ref = vmem
    copies = load((x, forward, inner, twiddle, taps, outer, backward), vmem, sems)
    copies[0].wait()
    copies[1].wait()
    coarse_forward(x_ref, forward_ref, mid_ref)
    for c in copies[2:6]:
        c.wait()

    def step(k, carry):
        value = fine_forward(mid_ref, twiddle_ref, inner_ref, k)
        spec_ref[k] = value
        copy(spec_ref.at[k], spec.at[k], out_sems.at[k]).start()
        fine_backward(mid_ref, twiddle_ref, outer_ref, k, times_conj(value, taps_ref[k]))
        return carry

    lax.fori_loop(0, coarse // 2, step, 0, unroll=unrolled)
    copies[6].wait()
    coarse_backward(mid_ref, backward_ref, y_ref, y, sems)

    def finish(k, carry):
        copy(spec_ref.at[k], spec.at[k], out_sems.at[k]).wait()
        return carry

    lax.fori_loop(0, coarse // 2, finish, 0)


def cross_kernel(x, forward, inner, twiddle, prod, outer, backward, y, *scratch):
    vmem, (y_ref, mid_ref, sems) = scratch[:7], scratch[7:]
    x_ref, forward_ref, inner_ref, twiddle_ref, prod_ref, outer_ref, backward_ref = vmem
    copies = load((x, forward, inner, twiddle, prod, outer, backward), vmem, sems)
    copies[0].wait()
    copies[1].wait()
    coarse_forward(x_ref, forward_ref, mid_ref)
    for c in copies[2:6]:
        c.wait()

    def step(k, carry):
        value = fine_forward(mid_ref, twiddle_ref, inner_ref, k)
        fine_backward(mid_ref, twiddle_ref, outer_ref, k, times_conj(prod_ref[k], value))
        return carry

    lax.fori_loop(0, coarse // 2, step, 0, unroll=unrolled)
    copies[6].wait()
    coarse_backward(mid_ref, backward_ref, y_ref, y, sems)


block_shape = (coarse, fine, fine)
spec_shape = jax.ShapeDtypeStruct((coarse // 2, 2 * fine, 2 * fine), f32)
params = pltpu.CompilerParams(vmem_limit_bytes=vmem_limit)
anywhere = pl.BlockSpec(memory_space=pl.ANY)


def call(kernel, out_shape, flops, *args):
    results = jax.tree.leaves(out_shape)
    scratch = [pltpu.VMEM(a.shape, a.dtype) for a in list(args) + results]
    scratch += [pltpu.VMEM((2 * coarse, fine, fine), f32), pltpu.SemaphoreType.DMA((8,))]
    if spec_shape in results:
        scratch.append(pltpu.SemaphoreType.DMA((coarse // 2,)))
    return pl.pallas_call(
        kernel,
        out_shape=out_shape,
        in_specs=[anywhere] * len(args),
        out_specs=jax.tree.map(lambda _: anywhere, out_shape),
        scratch_shapes=scratch,
        compiler_params=params,
        cost_estimate=pl.CostEstimate(flops=flops, bytes_accessed=2**23, transcendentals=0),
    )(*args)


def product_kernel(grad_ref, query_ref, out_ref):
    value = (grad_ref[0].astype(f32) * query_ref[0].astype(f32)).astype(bf16)
    for i in range(out_ref.shape[0]):
        out_ref[i] = value[:, i * fine : (i + 1) * fine]


def block_kernel(value_ref, out_ref):
    for i in range(out_ref.shape[0]):
        out_ref[i] = value_ref[0, :, i * fine : (i + 1) * fine]


def unblock_kernel(value_ref, out_ref):
    for i in range(value_ref.shape[0]):
        out_ref[0, :, i * fine : (i + 1) * fine] = value_ref[i]


blocks_a_step = 16


def to_blocks(kernel, *args):
    wide = pl.BlockSpec((1, fine, blocks_a_step * fine), lambda i: (0, 0, i))
    return pl.pallas_call(
        kernel,
        grid=(coarse // blocks_a_step,),
        in_specs=[wide] * len(args),
        out_specs=pl.BlockSpec((blocks_a_step, fine, fine), lambda i: (i, 0, 0)),
        out_shape=jax.ShapeDtypeStruct((coarse, fine, fine), bf16),
        compiler_params=params,
    )(*args)


def from_blocks(value):
    return pl.pallas_call(
        unblock_kernel,
        grid=(coarse // blocks_a_step,),
        in_specs=[pl.BlockSpec((blocks_a_step, fine, fine), lambda i: (i, 0, 0))],
        out_specs=pl.BlockSpec((1, fine, blocks_a_step * fine), lambda i: (0, 0, i)),
        out_shape=jax.ShapeDtypeStruct((1, fine, coarse * fine), bf16),
        compiler_params=params,
    )(value)


def to_owners(blocks):
    return lax.all_to_all(blocks, "ctx", 0, 0, tiled=True)


def swap(value, bit):
    return lax.ppermute(value, "dp", [(i, i ^ bit) for i in range(16)])


def turn(value, by):
    return lax.ppermute(value, "dp", [(i, (i + 4 * by) % 16) for i in range(16)])


def place():
    index = lax.axis_index("dp")
    return index // 4, index // 2 % 2, index % 2


def pair(mine, other, bit):
    return jnp.where(bit == 0, jnp.stack([mine, other]), jnp.stack([other, mine]))


def gather_taps(both):
    y, _, core = place()
    both = pair(both, swap(both, 1), core)
    both = jnp.transpose(both, (1, 0, 2, 3))
    whole = jnp.zeros((4,) + both.shape, both.dtype)
    whole = lax.dynamic_update_index_in_dim(whole, both, y, 0)
    for by in (1, 3, 2):
        whole = lax.dynamic_update_index_in_dim(whole, turn(both, by), (y - by) % 4, 0)
    return whole.reshape(coarse, fine, fine)


def sum_over_dp(cross):
    y, z_hi, core = place()
    parts = cross.reshape(4, 2, 2, 256, fine)
    away = lax.dynamic_index_in_dim(parts, 1 - core, 2, keepdims=False)
    kept = lax.dynamic_index_in_dim(parts, core, 2, keepdims=False) + swap(away, 1)
    total = lax.dynamic_index_in_dim(kept, y, 0, keepdims=False)
    for by in (1, 3, 2):
        away = lax.dynamic_index_in_dim(kept, (y + by) % 4, 0, keepdims=False)
        total = total + turn(away.astype(bf16), by).astype(f32)
    away = lax.dynamic_index_in_dim(total, 1 - z_hi, 0, keepdims=False)
    return lax.dynamic_index_in_dim(total, z_hi, 0, keepdims=False) + swap(away.astype(bf16), 2).astype(f32)


def body(query_act, gated_input, out_grad, filter_taps):
    forward, backward, twiddle, inner, outer = (jnp.asarray(t) for t in make_tables())
    taps = filter_taps.astype(bf16)
    other = swap(taps, 2)
    product = to_owners(to_blocks(product_kernel, out_grad, query_act))
    gated = to_blocks(block_kernel, gated_input)
    product, other, gated = lax.optimization_barrier((product, other, gated))
    taps = gather_taps(pair(taps, other, place()[1]))
    one = 2 * 256 * 256 * 256 * 32
    taps_spec = call(spectrum_kernel, spec_shape, 3 * one, taps, forward, inner, twiddle)
    gated = to_owners(gated)
    grad_rows, prod_spec = call(
        grad_kernel,
        (jax.ShapeDtypeStruct((coarse, fine, fine), bf16), spec_shape),
        6 * one,
        product, forward, inner, twiddle, taps_spec, outer, backward,
    )
    input_grad = from_blocks(to_owners(grad_rows))
    cross = call(
        cross_kernel,
        jax.ShapeDtypeStruct((coarse, fine, fine), f32),
        6 * one,
        gated, forward, inner, twiddle, prod_spec, outer, backward,
    )
    return input_grad, sum_over_dp(cross) * (1.0 / 256.0)


def solution(mesh):
    in_specs = (P("dp", "ctx", None), P("dp", "ctx", None), P("dp", "ctx", None), P("dp", "ctx"))
    out_specs = (P("dp", "ctx", None), P("dp", "ctx"))
    return jax.shard_map(body, mesh=mesh, in_specs=in_specs, out_specs=out_specs, check_vma=False)
```

time: 289 us -> 200 us (0.69)
  the two profiles are of different devices: /device:TPU:195 before, /device:TPU:56 now
where the time goes in v2:
time: 200 us
  waiting for transfers between devices  91.1 us (46%)
  starting transfers between devices  65.2 us (33%)
  Pallas kernels  36.3 us (18%)
  local copies, waits for them, and re-layouts  3.73 us (2%)
  other arithmetic  2.16 us (1%)
    all_to_all x3, waiting for transfers between devices, to_owners(): return lax.all_to_all(blocks, 'ctx', 0, 0, tiled=True)  66.7 us
    pallas_call x3, Pallas kernels, call(): pl.pallas_call(kernel, out_shape=out_shape, in_specs=[anywhere] * len(arg...  29.5 us
    all_to_all x3, starting transfers between devices, to_owners(): return lax.all_to_all(blocks, 'ctx', 0, 0, tiled=True)  28.6 us
    ppermute x4, starting transfers between devices, swap(): return lax.ppermute(value, 'dp', [(i, i ^ bit) for i in range(16)])  18.7 us
    ppermute x6, starting transfers between devices, turn(): lax.ppermute(value, 'dp', [(i, (i + 4 * by) % 16) for i in range(16)])  18 us
    ppermute x6, waiting for transfers between devices, turn(): lax.ppermute(value, 'dp', [(i, (i + 4 * by) % 16) for i in range(16)])  14.9 us
    ppermute x4, waiting for transfers between devices, swap(): return lax.ppermute(value, 'dp', [(i, i ^ bit) for i in range(16)])  9.47 us
    pallas_call x2, Pallas kernels, to_blocks(): pl.pallas_call(kernel, grid=(coarse // blocks_a_step,), in_specs=[wide] *...  4.68 us
  transfers between devices with their start and end apart: 13, of which 10 were waited for; matrix products, arithmetic and copies ran while one was open for 2% of the time, Pallas kernels for 17%

profile of v2, /device:TPU:56, one launch (start us, length us, event | category | flops | bytes accessed | tf_op | source)
XLA Modules:
  0.0 199.6 jit_solution(9783243550572375045)
XLA Ops:
  0.6 2.5 %shard_map.104 = bf16[32,128,128]{2,1,0:T(8,128)(2,1)} custom-call(bf16[1,128,4096]{2,1,0:T(8,128)(2,1)} %grad_ref.1, bf16[1,128,4096]{2,1,0:T(8,128)(2,1)} %query_ref.1), custom_call_target="tpu_custom_call" | custom-call | tf_op jit(solution)/shard_map/pallas_call | solution.py:246
  3.1 15.2 %all-to-all-start = ((bf16[32,128,128]{2,1,0:T(8,128)(2,1)}), bf16[32,128,128]{2,1,0:T(8,128)(2,1)S(1)}, u32[]{:S(2)}, u32[]{:S(2)}) async-start(bf16[32,128,128]{2,1,0:T(8,128)(2,1)} %shard_map.104), calls=%async_computation | async-start | bytes 2097152 | tf_op jit(solution)/shard_map/all_to_all | solution.py:268
  18.4 8.2 %collective-permute-start = (bf16[256,128]{1,0:T(8,128)(2,1)S(1)}, bf16[256,128]{1,0:T(8,128)(2,1)S(1)}, u32[]{:S(2)}, u32[]{:S(2)}) collective-permute-start(bf16[256,128]{1,0:T(8,128)(2,1)S(1)} %convert_element_type.39), channel_id=1, source_target_pairs={{0,64},{32,96},{64,0},{96,32},{128,192},{160,224},{192,128},{224,1... | collective-permute-start | bytes 196616 | tf_op jit(solution)/shard_map/ppermute | solution.py:272
  26.6 2.2 %shard_map.105 = bf16[32,128,128]{2,1,0:T(8,128)(2,1)} custom-call(bf16[1,128,4096]{2,1,0:T(8,128)(2,1)} %value_ref.1), custom_call_target="tpu_custom_call" | custom-call | tf_op jit(solution)/shard_map/pallas_call | solution.py:246
  28.8 5.6 %collective-permute-done = bf16[256,128]{1,0:T(8,128)(2,1)S(1)} collective-permute-done((bf16[256,128]{1,0:T(8,128)(2,1)S(1)}, bf16[256,128]{1,0:T(8,128)(2,1)S(1)}, u32[]{:S(2)}, u32[]{:S(2)}) %collective-permute-start) | collective-permute-done | bytes 65568 | tf_op jit(solution)/shard_map/ppermute | solution.py:272
  34.5 41.2 %all-to-all-done.x = bf16[32,128,128]{2,1,0:T(8,128)(2,1)S(1)} async-done(((bf16[32,128,128]{2,1,0:T(8,128)(2,1)}), bf16[32,128,128]{2,1,0:T(8,128)(2,1)S(1)}, u32[]{:S(2)}, u32[]{:S(2)}) %all-to-all-start) | async-done | bytes 1048608 | tf_op jit(solution)/shard_map/all_to_all | solution.py:268
  75.7 7.7 %all-to-all-start.2 = ((bf16[32,128,128]{2,1,0:T(8,128)(2,1)}), bf16[32,128,128]{2,1,0:T(8,128)(2,1)S(1)}, u32[]{:S(2)}, u32[]{:S(2)}) async-start(bf16[32,128,128]{2,1,0:T(8,128)(2,1)} %shard_map.105), calls=%async_computation.2 | async-start | bytes 2097152 | tf_op jit(solution)/shard_map/all_to_all | solution.py:268
  83.5 1.9 collective-permute-start.1
  85.5 1.3 collective-permute-done.1
  86.8 2.1 %collective-permute-start.2 = (bf16[2,2,256,128]{3,2,0,1:T(8,128)(2,1)S(1)}, bf16[2,2,256,128]{3,2,0,1:T(8,128)(2,1)S(1)}, u32[]{:S(2)}, u32[]{:S(2)}) collective-permute-start(bf16[2,2,256,128]{3,2,0,1:T(8,128)(2,1)S(1)} %get-tuple-element.15), channel_id=1, source_target_pairs={{0,128},{32,160},{64,192},{96,224},{128,256},{160,288},{192,320},{... | collective-permute-start | bytes 786440 | tf_op jit(solution)/shard_map/ppermute | solution.py:276
  89.0 3.7 %collective-permute-start.3 = (bf16[2,2,256,128]{3,2,0,1:T(8,128)(2,1)S(1)}, bf16[2,2,256,128]{3,2,0,1:T(8,128)(2,1)S(1)}, u32[]{:S(2)}, u32[]{:S(2)}) collective-permute-start(bf16[2,2,256,128]{3,2,0,1:T(8,128)(2,1)S(1)} %get-tuple-element.15), channel_id=1, source_target_pairs={{0,384},{32,416},{64,448},{96,480},{128,0},{160,32},{192,64},{224,... | collective-permute-start | bytes 786440 | tf_op jit(solution)/shard_map/ppermute | solution.py:276
  92.7 3.1 %collective-permute-start.4 = (bf16[2,2,256,128]{3,2,0,1:T(8,128)(2,1)S(1)}, bf16[2,2,256,128]{3,2,0,1:T(8,128)(2,1)S(1)}, u32[]{:S(2)}, u32[]{:S(2)}) collective-permute-start(bf16[2,2,256,128]{3,2,0,1:T(8,128)(2,1)S(1)} %get-tuple-element.15), channel_id=1, source_target_pairs={{0,256},{32,288},{64,320},{96,352},{128,384},{160,416},{192,448},{... | collective-permute-start | bytes 786440 | tf_op jit(solution)/shard_map/ppermute | solution.py:276
  97.1 8.8 %collective-permute-done.3 = bf16[2,2,256,128]{3,2,0,1:T(8,128)(2,1)S(1)} collective-permute-done((bf16[2,2,256,128]{3,2,0,1:T(8,128)(2,1)S(1)}, bf16[2,2,256,128]{3,2,0,1:T(8,128)(2,1)S(1)}, u32[]{:S(2)}, u32[]{:S(2)}) %collective-permute-start.3) | collective-permute-done | bytes 262176 | tf_op jit(solution)/shard_map/ppermute | solution.py:276
  106.0 1.0 copy-done.4
  107.0 6.4 %shard_map.106.taps = f32[16,256,256]{2,1,0:T(8,128)} custom-call(bf16[32,128,128]{2,1,0:T(8,128)(2,1)} %bitcast.47, bf16[512,768]{1,0:T(8,128)(2,1)} %constant.136.clone.forward, bf16[256,768]{1,0:T(8,128)(2,1)} %constant.139.clone.inner, f32[32,2,128,128]{3,2,1,0:T(8,128)} %constant.138.clone.twiddle), custom_call_target="tpu_custom_call" | custom-call | flops 3221225472 | bytes 8388608 | tf_op jit(solution)/shard_map/pallas_call | solution.py:214
  113.4 11.6 %shard_map.107 = (bf16[32,128,128]{2,1,0:T(8,128)(2,1)}, f32[16,256,256]{2,1,0:T(8,128)}) custom-call(bf16[32,128,128]{2,1,0:T(8,128)(2,1)} %copy-done.3, bf16[512,768]{1,0:T(8,128)(2,1)} %constant.136.clone.forward, bf16[256,768]{1,0:T(8,128)(2,1)} %constant.139.clone.inner, f32[32,2,128,128]{3,2,1,0:T(8,128)} %constant.138.clone.twiddle, ...), custom_call_target="tpu_custom_call" | custom-call | flops 6442450944 | bytes 8388608 | tf_op jit(solution)/shard_map/pallas_call | solution.py:214
  125.1 9.0 %all-to-all-done.2.x = bf16[32,128,128]{2,1,0:T(8,128)(2,1)S(1)} async-done(((bf16[32,128,128]{2,1,0:T(8,128)(2,1)}), bf16[32,128,128]{2,1,0:T(8,128)(2,1)S(1)}, u32[]{:S(2)}, u32[]{:S(2)}) %all-to-all-start.2) | async-done | bytes 1048608 | tf_op jit(solution)/shard_map/all_to_all | solution.py:268
  134.0 5.6 %all-to-all-start.1 = ((bf16[32,128,128]{2,1,0:T(8,128)(2,1)}), bf16[32,128,128]{2,1,0:T(8,128)(2,1)S(1)}, u32[]{:S(2)}, u32[]{:S(2)}) async-start(bf16[32,128,128]{2,1,0:T(8,128)(2,1)} %get-tuple-element.9), calls=%async_computation.1 | async-start | bytes 2097152 | tf_op jit(solution)/shard_map/all_to_all | solution.py:268
  139.7 11.4 %shard_map.109 = f32[32,128,128]{2,1,0:T(8,128)} custom-call(bf16[32,128,128]{2,1,0:T(8,128)(2,1)} %copy-done.2, bf16[512,768]{1,0:T(8,128)(2,1)} %constant.136.clone.forward, bf16[256,768]{1,0:T(8,128)(2,1)} %constant.139.clone.inner, f32[32,2,128,128]{3,2,1,0:T(8,128)} %constant.138.clone.twiddle, f32[16,256,256]{2,1,0:T(8,128)} %get-tuple-element.11.prod, ...), custom_call_target="tpu_custom_call" | custom-call | flops 6442450944 | bytes 8388608 | tf_op jit(solution)/shard_map/pallas_call | solution.py:214
  151.1 1.3 dynamic-slice_bitcast_fusion
  152.4 1.9 collective-permute-start.5
  154.4 2.6 %collective-permute-done.5 = f32[4,2,256,128]{3,2,1,0:T(8,128)S(1)} collective-permute-done((f32[4,2,256,128]{3,2,1,0:T(8,128)S(1)}, f32[4,2,256,128]{3,2,1,0:T(8,128)S(1)}, u32[]{:S(2)}, u32[]{:S(2)}) %collective-permute-start.5) | collective-permute-done | bytes 1048608 | tf_op jit(solution)/shard_map/ppermute | solution.py:272
  156.9 1.3 bitcast_add_fusion
  158.4 2.1 %collective-permute-start.6 = (bf16[2,256,128]{2,1,0:T(8,128)(2,1)S(1)}, bf16[2,256,128]{2,1,0:T(8,128)(2,1)S(1)}, u32[]{:S(2)}, u32[]{:S(2)}) collective-permute-start(bf16[2,256,128]{2,1,0:T(8,128)(2,1)S(1)} %get-tuple-element.12), channel_id=1, source_target_pairs={{0,128},{32,160},{64,192},{96,224},{128,256},{160,288},{192,320},{... | collective-permute-start | bytes 393224 | tf_op jit(solution)/shard_map/ppermute | solution.py:276
  160.5 3.7 %collective-permute-start.7 = (bf16[2,256,128]{2,1,0:T(8,128)(2,1)S(1)}, bf16[2,256,128]{2,1,0:T(8,128)(2,1)S(1)}, u32[]{:S(2)}, u32[]{:S(2)}) collective-permute-start(bf16[2,256,128]{2,1,0:T(8,128)(2,1)S(1)} %get-tuple-element.14), channel_id=1, source_target_pairs={{0,384},{32,416},{64,448},{96,480},{128,0},{160,32},{192,64},{224,... | collective-permute-start | bytes 393224 | tf_op jit(solution)/shard_map/ppermute | solution.py:276
  164.2 3.1 %collective-permute-start.8 = (bf16[2,256,128]{2,1,0:T(8,128)(2,1)S(1)}, bf16[2,256,128]{2,1,0:T(8,128)(2,1)S(1)}, u32[]{:S(2)}, u32[]{:S(2)}) collective-permute-start(bf16[2,256,128]{2,1,0:T(8,128)(2,1)S(1)} %get-tuple-element.13), channel_id=1, source_target_pairs={{0,256},{32,288},{64,320},{96,352},{128,384},{160,416},{192,448},{... | collective-permute-start | bytes 393224 | tf_op jit(solution)/shard_map/ppermute | solution.py:276
  167.4 1.5 collective-permute-done.7
  168.9 3.7 %collective-permute-done.8 = bf16[2,256,128]{2,1,0:T(8,128)(2,1)S(1)} collective-permute-done((bf16[2,256,128]{2,1,0:T(8,128)(2,1)S(1)}, bf16[2,256,128]{2,1,0:T(8,128)(2,1)S(1)}, u32[]{:S(2)}, u32[]{:S(2)}) %collective-permute-start.8) | collective-permute-done | bytes 131104 | tf_op jit(solution)/shard_map/ppermute | solution.py:276
  172.7 6.6 %collective-permute-start.9 = (bf16[256,128]{1,0:T(8,128)(2,1)S(1)}, bf16[256,128]{1,0:T(8,128)(2,1)S(1)}, u32[]{:S(2)}, u32[]{:S(2)}) collective-permute-start(bf16[256,128]{1,0:T(8,128)(2,1)S(1)} %fusion.6), channel_id=1, source_target_pairs={{0,64},{32,96},{64,0},{96,32},{128,192},{160,224},{192,128},{224,1... | collective-permute-start | bytes 196616 | tf_op jit(solution)/shard_map/ppermute | solution.py:272
  179.3 16.5 %all-to-all-done.1.value_ref = bf16[32,128,128]{2,1,0:T(8,128)(2,1)S(1)} async-done(((bf16[32,128,128]{2,1,0:T(8,128)(2,1)}), bf16[32,128,128]{2,1,0:T(8,128)(2,1)S(1)}, u32[]{:S(2)}, u32[]{:S(2)}) %all-to-all-start.1) | async-done | bytes 1048608 | tf_op jit(solution)/shard_map/all_to_all | solution.py:268
  195.8 1.0 copy-done
  196.8 2.1 %shard_map.108 = bf16[1,128,4096]{2,1,0:T(8,128)(2,1)} custom-call(bf16[32,128,128]{2,1,0:T(8,128)(2,1)} %copy-done), custom_call_target="tpu_custom_call" | custom-call | tf_op jit(solution)/shard_map/pallas_call | solution.py:257
  (27 shorter events, 2.2 us)
Async XLA Ops:
  0.6 17.7 %copy-start.1 = (f32[256,128]{1,0:T(8,128)S(1)}, f32[256,128]{1,0:T(8,128)}, u32[]{:S(2)}) copy-start(f32[256,128]{1,0:T(8,128)} %param.12) | copy-start | bytes 393220
  3.1 72.6 %all-to-all-start = ((bf16[32,128,128]{2,1,0:T(8,128)(2,1)}), bf16[32,128,128]{2,1,0:T(8,128)(2,1)S(1)}, u32[]{:S(2)}, u32[]{:S(2)}) async-start(bf16[32,128,128]{2,1,0:T(8,128)(2,1)} %shard_map.104), calls=%async_computation | async-start | bytes 2097152 | tf_op jit(solution)/shard_map/all_to_all | solution.py:268
  18.4 16.1 %collective-permute-start = (bf16[256,128]{1,0:T(8,128)(2,1)S(1)}, bf16[256,128]{1,0:T(8,128)(2,1)S(1)}, u32[]{:S(2)}, u32[]{:S(2)}) collective-permute-start(bf16[256,128]{1,0:T(8,128)(2,1)S(1)} %convert_element_type.39), channel_id=1, source_target_pairs={{0,64},{32,96},{64,0},{96,32},{128,192},{160,224},{192,128},{224,1... | collective-permute-start | bytes 196616 | tf_op jit(solution)/shard_map/ppermute | solution.py:272
  75.7 37.7 %copy-start.3 = (bf16[32,128,128]{2,1,0:T(8,128)(2,1)}, bf16[32,128,128]{2,1,0:T(8,128)(2,1)S(1)}, u32[]{:S(2)}) copy-start(bf16[32,128,128]{2,1,0:T(8,128)(2,1)S(1)} %all-to-all-done.x) | copy-start | bytes 3145732
  75.7 58.3 %all-to-all-start.2 = ((bf16[32,128,128]{2,1,0:T(8,128)(2,1)}), bf16[32,128,128]{2,1,0:T(8,128)(2,1)S(1)}, u32[]{:S(2)}, u32[]{:S(2)}) async-start(bf16[32,128,128]{2,1,0:T(8,128)(2,1)} %shard_map.105), calls=%async_computation.2 | async-start | bytes 2097152 | tf_op jit(solution)/shard_map/all_to_all | solution.py:268
  83.5 3.2 %collective-permute-start.1 = (bf16[2,256,128]{2,1,0:T(8,128)(2,1)S(1)}, bf16[2,256,128]{2,1,0:T(8,128)(2,1)S(1)}, u32[]{:S(2)}, u32[]{:S(2)}) collective-permute-start(bf16[2,256,128]{2,1,0:T(8,128)(2,1)S(1)} %maximum_select_fusion.2), channel_id=1, source_target_pairs={{0,32},{32,0},{64,96},{96,64},{128,160},{160,128},{192,224},{224,1... | collective-permute-start | bytes 393224 | tf_op jit(solution)/shard_map/ppermute | solution.py:272
  86.8 10.3 %collective-permute-start.2 = (bf16[2,2,256,128]{3,2,0,1:T(8,128)(2,1)S(1)}, bf16[2,2,256,128]{3,2,0,1:T(8,128)(2,1)S(1)}, u32[]{:S(2)}, u32[]{:S(2)}) collective-permute-start(bf16[2,2,256,128]{3,2,0,1:T(8,128)(2,1)S(1)} %get-tuple-element.15), channel_id=1, source_target_pairs={{0,128},{32,160},{64,192},{96,224},{128,256},{160,288},{192,320},{... | collective-permute-start | bytes 786440 | tf_op jit(solution)/shard_map/ppermute | solution.py:276
  89.0 16.9 %collective-permute-start.3 = (bf16[2,2,256,128]{3,2,0,1:T(8,128)(2,1)S(1)}, bf16[2,2,256,128]{3,2,0,1:T(8,128)(2,1)S(1)}, u32[]{:S(2)}, u32[]{:S(2)}) collective-permute-start(bf16[2,2,256,128]{3,2,0,1:T(8,128)(2,1)S(1)} %get-tuple-element.15), channel_id=1, source_target_pairs={{0,384},{32,416},{64,448},{96,480},{128,0},{160,32},{192,64},{224,... | collective-permute-start | bytes 786440 | tf_op jit(solution)/shard_map/ppermute | solution.py:276
  92.7 13.2 %collective-permute-start.4 = (bf16[2,2,256,128]{3,2,0,1:T(8,128)(2,1)S(1)}, bf16[2,2,256,128]{3,2,0,1:T(8,128)(2,1)S(1)}, u32[]{:S(2)}, u32[]{:S(2)}) collective-permute-start(bf16[2,2,256,128]{3,2,0,1:T(8,128)(2,1)S(1)} %get-tuple-element.15), channel_id=1, source_target_pairs={{0,256},{32,288},{64,320},{96,352},{128,384},{160,416},{192,448},{... | collective-permute-start | bytes 786440 | tf_op jit(solution)/shard_map/ppermute | solution.py:276
  106.0 1.0 copy-start.4
  134.0 5.6 %copy-start.2 = (bf16[32,128,128]{2,1,0:T(8,128)(2,1)}, bf16[32,128,128]{2,1,0:T(8,128)(2,1)S(1)}, u32[]{:S(2)}) copy-start(bf16[32,128,128]{2,1,0:T(8,128)(2,1)S(1)} %all-to-all-done.2.x) | copy-start | bytes 3145732
  134.0 61.8 %all-to-all-start.1 = ((bf16[32,128,128]{2,1,0:T(8,128)(2,1)}), bf16[32,128,128]{2,1,0:T(8,128)(2,1)S(1)}, u32[]{:S(2)}, u32[]{:S(2)}) async-start(bf16[32,128,128]{2,1,0:T(8,128)(2,1)} %get-tuple-element.9), calls=%async_computation.1 | async-start | bytes 2097152 | tf_op jit(solution)/shard_map/all_to_all | solution.py:268
  152.4 4.6 %collective-permute-start.5 = (f32[4,2,256,128]{3,2,1,0:T(8,128)S(1)}, f32[4,2,256,128]{3,2,1,0:T(8,128)S(1)}, u32[]{:S(2)}, u32[]{:S(2)}) collective-permute-start(f32[4,2,256,128]{3,2,1,0:T(8,128)S(1)} %dynamic-slice_bitcast_fusion), channel_id=1, source_target_pairs={{0,32},{32,0},{64,96},{96,64},{128,160},{160,128},{192,224},{224,1... | collective-permute-start | bytes 3145736 | tf_op jit(solution)/shard_map/ppermute | solution.py:272
  158.4 9.0 %collective-permute-start.6 = (bf16[2,256,128]{2,1,0:T(8,128)(2,1)S(1)}, bf16[2,256,128]{2,1,0:T(8,128)(2,1)S(1)}, u32[]{:S(2)}, u32[]{:S(2)}) collective-permute-start(bf16[2,256,128]{2,1,0:T(8,128)(2,1)S(1)} %get-tuple-element.12), channel_id=1, source_target_pairs={{0,128},{32,160},{64,192},{96,224},{128,256},{160,288},{192,320},{... | collective-permute-start | bytes 393224 | tf_op jit(solution)/shard_map/ppermute | solution.py:276
  160.5 8.4 %collective-permute-start.7 = (bf16[2,256,128]{2,1,0:T(8,128)(2,1)S(1)}, bf16[2,256,128]{2,1,0:T(8,128)(2,1)S(1)}, u32[]{:S(2)}, u32[]{:S(2)}) collective-permute-start(bf16[2,256,128]{2,1,0:T(8,128)(2,1)S(1)} %get-tuple-element.14), channel_id=1, source_target_pairs={{0,384},{32,416},{64,448},{96,480},{128,0},{160,32},{192,64},{224,... | collective-permute-start | bytes 393224 | tf_op jit(solution)/shard_map/ppermute | solution.py:276
  164.2 8.4 %collective-permute-start.8 = (bf16[2,256,128]{2,1,0:T(8,128)(2,1)S(1)}, bf16[2,256,128]{2,1,0:T(8,128)(2,1)S(1)}, u32[]{:S(2)}, u32[]{:S(2)}) collective-permute-start(bf16[2,256,128]{2,1,0:T(8,128)(2,1)S(1)} %get-tuple-element.13), channel_id=1, source_target_pairs={{0,256},{32,288},{64,320},{96,352},{128,384},{160,416},{192,448},{... | collective-permute-start | bytes 393224 | tf_op jit(solution)/shard_map/ppermute | solution.py:276
  172.7 26.3 %collective-permute-start.9 = (bf16[256,128]{1,0:T(8,128)(2,1)S(1)}, bf16[256,128]{1,0:T(8,128)(2,1)S(1)}, u32[]{:S(2)}, u32[]{:S(2)}) collective-permute-start(bf16[256,128]{1,0:T(8,128)(2,1)S(1)} %fusion.6), channel_id=1, source_target_pairs={{0,64},{32,96},{64,0},{96,32},{128,192},{160,224},{192,128},{224,1... | collective-permute-start | bytes 196616 | tf_op jit(solution)/shard_map/ppermute | solution.py:272
  195.8 1.0 copy-start

commit v3 on v2

--- a/solution.py
+++ b/solution.py
@@ -233,11 +233,6 @@
         out_ref[i] = value_ref[0, :, i * fine : (i + 1) * fine]
 
 
-def unblock_kernel(value_ref, out_ref):
-    for i in range(value_ref.shape[0]):
-        out_ref[0, :, i * fine : (i + 1) * fine] = value_ref[i]
-
-
 blocks_a_step = 16
 
 
@@ -254,14 +249,7 @@
 
 
 def from_blocks(value):
-    return pl.pallas_call(
-        unblock_kernel,
-        grid=(coarse // blocks_a_step,),
-        in_specs=[pl.BlockSpec((blocks_a_step, fine, fine), lambda i: (i, 0, 0))],
-        out_specs=pl.BlockSpec((1, fine, blocks_a_step * fine), lambda i: (0, 0, i)),
-        out_shape=jax.ShapeDtypeStruct((1, fine, coarse * fine), bf16),
-        compiler_params=params,
-    )(value)
+    return jnp.transpose(value, (1, 0, 2)).reshape(1, fine, coarse * fine)
 
 
 def to_owners(blocks):
@@ -300,7 +288,7 @@
     y, z_hi, core = place()
     parts = cross.reshape(4, 2, 2, 256, fine)
     away = lax.dynamic_index_in_dim(parts, 1 - core, 2, keepdims=False)
-    kept = lax.dynamic_index_in_dim(parts, core, 2, keepdims=False) + swap(away, 1)
+    kept = lax.dynamic_index_in_dim(parts, core, 2, keepdims=False) + swap(away.astype(bf16), 1).astype(f32)
     total = lax.dynamic_index_in_dim(kept, y, 0, keepdims=False)
     for by in (1, 3, 2):
         away = lax.dynamic_index_in_dim(kept, (y + by) % 4, 0, keepdims=False)

time: 200 us -> 199 us (level)
  Pallas kernels: 36.3 us -> 34.2 us
    pallas_call x1 -> x0, Pallas kernels: 2.14 us -> none  [from_blocks(): pl.pallas_call(unblock_kernel, grid=(coarse // blocks_a_step,), in_specs=...]
  transfers between devices with their start and end apart: 13 -> 13, of which waited for: 10 -> 10; matrix products, arithmetic and copies ran while one was open for 2% -> 3% of each run, Pallas kernels for 17% -> 16%
where the time goes in v3:
time: 199 us
  waiting for transfers between devices  91.1 us (46%)
  starting transfers between devices  65.2 us (33%)
  Pallas kernels  34.2 us (17%)
  local copies, waits for them, and re-layouts  4.72 us (2%)
  other arithmetic  2.14 us (1%)
    all_to_all x3, waiting for transfers between devices, to_owners(): return lax.all_to_all(blocks, 'ctx', 0, 0, tiled=True)  67.5 us
    pallas_call x3, Pallas kernels, call(): pl.pallas_call(kernel, out_shape=out_shape, in_specs=[anywhere] * len(arg...  29.5 us
    all_to_all x3, starting transfers between devices, to_owners(): return lax.all_to_all(blocks, 'ctx', 0, 0, tiled=True)  28.6 us
    ppermute x4, starting transfers between devices, swap(): return lax.ppermute(value, 'dp', [(i, i ^ bit) for i in range(16)])  18.7 us
    ppermute x6, starting transfers between devices, turn(): lax.ppermute(value, 'dp', [(i, (i + 4 * by) % 16) for i in range(16)])  18 us
    ppermute x6, waiting for transfers between devices, turn(): lax.ppermute(value, 'dp', [(i, (i + 4 * by) % 16) for i in range(16)])  14.9 us
    ppermute x4, waiting for transfers between devices, swap(): return lax.ppermute(value, 'dp', [(i, i ^ bit) for i in range(16)])  8.71 us
    pallas_call x2, Pallas kernels, to_blocks(): pl.pallas_call(kernel, grid=(coarse // blocks_a_step,), in_specs=[wide] *...  4.68 us
  transfers between devices with their start and end apart: 13, of which 10 were waited for; matrix products, arithmetic and copies ran while one was open for 3% of the time, Pallas kernels for 16%

profile of v3, /device:TPU:56, one launch (start us, length us, event | category | flops | bytes accessed | tf_op | source)
XLA Modules:
  0.0 198.5 jit_solution(546984392127018297)
XLA Ops:
  0.6 2.5 %shard_map.104 = bf16[32,128,128]{2,1,0:T(8,128)(2,1)} custom-call(bf16[1,128,4096]{2,1,0:T(8,128)(2,1)} %grad_ref.1, bf16[1,128,4096]{2,1,0:T(8,128)(2,1)} %query_ref.1), custom_call_target="tpu_custom_call" | custom-call | tf_op jit(solution)/shard_map/pallas_call | solution.py:241
  3.1 15.2 %all-to-all-start = ((bf16[32,128,128]{2,1,0:T(8,128)(2,1)}), bf16[32,128,128]{2,1,0:T(8,128)(2,1)S(1)}, u32[]{:S(2)}, u32[]{:S(2)}) async-start(bf16[32,128,128]{2,1,0:T(8,128)(2,1)} %shard_map.104), calls=%async_computation | async-start | bytes 2097152 | tf_op jit(solution)/shard_map/all_to_all | solution.py:256
  18.4 8.2 %collective-permute-start = (bf16[256,128]{1,0:T(8,128)(2,1)S(1)}, bf16[256,128]{1,0:T(8,128)(2,1)S(1)}, u32[]{:S(2)}, u32[]{:S(2)}) collective-permute-start(bf16[256,128]{1,0:T(8,128)(2,1)S(1)} %convert_element_type.48), channel_id=1, source_target_pairs={{0,64},{32,96},{64,0},{96,32},{128,192},{160,224},{192,128},{224,1... | collective-permute-start | bytes 196616 | tf_op jit(solution)/shard_map/ppermute | solution.py:260
  26.6 2.2 %shard_map.105 = bf16[32,128,128]{2,1,0:T(8,128)(2,1)} custom-call(bf16[1,128,4096]{2,1,0:T(8,128)(2,1)} %value_ref.1), custom_call_target="tpu_custom_call" | custom-call | tf_op jit(solution)/shard_map/pallas_call | solution.py:241
  28.8 5.6 %collective-permute-done = bf16[256,128]{1,0:T(8,128)(2,1)S(1)} collective-permute-done((bf16[256,128]{1,0:T(8,128)(2,1)S(1)}, bf16[256,128]{1,0:T(8,128)(2,1)S(1)}, u32[]{:S(2)}, u32[]{:S(2)}) %collective-permute-start) | collective-permute-done | bytes 65568 | tf_op jit(solution)/shard_map/ppermute | solution.py:260
  34.5 41.2 %all-to-all-done.x = bf16[32,128,128]{2,1,0:T(8,128)(2,1)S(1)} async-done(((bf16[32,128,128]{2,1,0:T(8,128)(2,1)}), bf16[32,128,128]{2,1,0:T(8,128)(2,1)S(1)}, u32[]{:S(2)}, u32[]{:S(2)}) %all-to-all-start) | async-done | bytes 1048608 | tf_op jit(solution)/shard_map/all_to_all | solution.py:256
  75.7 7.7 %all-to-all-start.2 = ((bf16[32,128,128]{2,1,0:T(8,128)(2,1)}), bf16[32,128,128]{2,1,0:T(8,128)(2,1)S(1)}, u32[]{:S(2)}, u32[]{:S(2)}) async-start(bf16[32,128,128]{2,1,0:T(8,128)(2,1)} %shard_map.105), calls=%async_computation.2 | async-start | bytes 2097152 | tf_op jit(solution)/shard_map/all_to_all | solution.py:256
  83.5 1.9 collective-permute-start.1
  85.5 1.3 collective-permute-done.1
  86.8 2.1 %collective-permute-start.2 = (bf16[2,2,256,128]{3,2,0,1:T(8,128)(2,1)S(1)}, bf16[2,2,256,128]{3,2,0,1:T(8,128)(2,1)S(1)}, u32[]{:S(2)}, u32[]{:S(2)}) collective-permute-start(bf16[2,2,256,128]{3,2,0,1:T(8,128)(2,1)S(1)} %get-tuple-element.17), channel_id=1, source_target_pairs={{0,128},{32,160},{64,192},{96,224},{128,256},{160,288},{192,320},{... | collective-permute-start | bytes 786440 | tf_op jit(solution)/shard_map/ppermute | solution.py:264
  89.0 3.7 %collective-permute-start.3 = (bf16[2,2,256,128]{3,2,0,1:T(8,128)(2,1)S(1)}, bf16[2,2,256,128]{3,2,0,1:T(8,128)(2,1)S(1)}, u32[]{:S(2)}, u32[]{:S(2)}) collective-permute-start(bf16[2,2,256,128]{3,2,0,1:T(8,128)(2,1)S(1)} %get-tuple-element.17), channel_id=1, source_target_pairs={{0,384},{32,416},{64,448},{96,480},{128,0},{160,32},{192,64},{224,... | collective-permute-start | bytes 786440 | tf_op jit(solution)/shard_map/ppermute | solution.py:264
  92.7 3.1 %collective-permute-start.4 = (bf16[2,2,256,128]{3,2,0,1:T(8,128)(2,1)S(1)}, bf16[2,2,256,128]{3,2,0,1:T(8,128)(2,1)S(1)}, u32[]{:S(2)}, u32[]{:S(2)}) collective-permute-start(bf16[2,2,256,128]{3,2,0,1:T(8,128)(2,1)S(1)} %get-tuple-element.17), channel_id=1, source_target_pairs={{0,256},{32,288},{64,320},{96,352},{128,384},{160,416},{192,448},{... | collective-permute-start | bytes 786440 | tf_op jit(solution)/shard_map/ppermute | solution.py:264
  96.1 0.9 collective-permute-done.2
  97.1 8.8 %collective-permute-done.3 = bf16[2,2,256,128]{3,2,0,1:T(8,128)(2,1)S(1)} collective-permute-done((bf16[2,2,256,128]{3,2,0,1:T(8,128)(2,1)S(1)}, bf16[2,2,256,128]{3,2,0,1:T(8,128)(2,1)S(1)}, u32[]{:S(2)}, u32[]{:S(2)}) %collective-permute-start.3) | collective-permute-done | bytes 262176 | tf_op jit(solution)/shard_map/ppermute | solution.py:264
  106.0 1.0 copy-done.3
  107.0 6.4 %shard_map.106.taps = f32[16,256,256]{2,1,0:T(8,128)} custom-call(bf16[32,128,128]{2,1,0:T(8,128)(2,1)} %bitcast.55, bf16[512,768]{1,0:T(8,128)(2,1)} %constant.136.clone.forward, bf16[256,768]{1,0:T(8,128)(2,1)} %constant.139.clone.inner, f32[32,2,128,128]{3,2,1,0:T(8,128)} %constant.138.clone.twiddle), custom_call_target="tpu_custom_call" | custom-call | flops 3221225472 | bytes 8388608 | tf_op jit(solution)/shard_map/pallas_call | solution.py:214
  113.4 11.6 %shard_map.107 = (bf16[32,128,128]{2,1,0:T(8,128)(2,1)}, f32[16,256,256]{2,1,0:T(8,128)}) custom-call(bf16[32,128,128]{2,1,0:T(8,128)(2,1)} %copy-done.2, bf16[512,768]{1,0:T(8,128)(2,1)} %constant.136.clone.forward, bf16[256,768]{1,0:T(8,128)(2,1)} %constant.139.clone.inner, f32[32,2,128,128]{3,2,1,0:T(8,128)} %constant.138.clone.twiddle, ...), custom_call_target="tpu_custom_call" | custom-call | flops 6442450944 | bytes 8388608 | tf_op jit(solution)/shard_map/pallas_call | solution.py:214
  125.1 9.0 %all-to-all-done.2.x = bf16[32,128,128]{2,1,0:T(8,128)(2,1)S(1)} async-done(((bf16[32,128,128]{2,1,0:T(8,128)(2,1)}), bf16[32,128,128]{2,1,0:T(8,128)(2,1)S(1)}, u32[]{:S(2)}, u32[]{:S(2)}) %all-to-all-start.2) | async-done | bytes 1048608 | tf_op jit(solution)/shard_map/all_to_all | solution.py:256
  134.0 5.6 %all-to-all-start.1 = ((bf16[32,128,128]{2,1,0:T(8,128)(2,1)}), bf16[32,128,128]{2,1,0:T(8,128)(2,1)S(1)}, u32[]{:S(2)}, u32[]{:S(2)}) async-start(bf16[32,128,128]{2,1,0:T(8,128)(2,1)} %get-tuple-element.9), calls=%async_computation.1 | async-start | bytes 2097152 | tf_op jit(solution)/shard_map/all_to_all | solution.py:256
  139.7 11.4 %shard_map.108 = f32[32,128,128]{2,1,0:T(8,128)} custom-call(bf16[32,128,128]{2,1,0:T(8,128)(2,1)} %copy-done.1, bf16[512,768]{1,0:T(8,128)(2,1)} %constant.136.clone.forward, bf16[256,768]{1,0:T(8,128)(2,1)} %constant.139.clone.inner, f32[32,2,128,128]{3,2,1,0:T(8,128)} %constant.138.clone.twiddle, f32[16,256,256]{2,1,0:T(8,128)} %get-tuple-element.11.prod, ...), custom_call_target="tpu_custom_call" | custom-call | flops 6442450944 | bytes 8388608 | tf_op jit(solution)/shard_map/pallas_call | solution.py:214
  151.1 1.3 fusion
  152.4 1.9 collective-permute-start.5
  154.4 1.8 collective-permute-done.5
  156.2 1.3 bitcast_add_fusion
  157.6 2.1 %collective-permute-start.6 = (bf16[2,256,128]{2,1,0:T(8,128)(2,1)S(1)}, bf16[2,256,128]{2,1,0:T(8,128)(2,1)S(1)}, u32[]{:S(2)}, u32[]{:S(2)}) collective-permute-start(bf16[2,256,128]{2,1,0:T(8,128)(2,1)S(1)} %get-tuple-element.14), channel_id=1, source_target_pairs={{0,128},{32,160},{64,192},{96,224},{128,256},{160,288},{192,320},{... | collective-permute-start | bytes 393224 | tf_op jit(solution)/shard_map/ppermute | solution.py:264
  159.8 3.7 %collective-permute-start.7 = (bf16[2,256,128]{2,1,0:T(8,128)(2,1)S(1)}, bf16[2,256,128]{2,1,0:T(8,128)(2,1)S(1)}, u32[]{:S(2)}, u32[]{:S(2)}) collective-permute-start(bf16[2,256,128]{2,1,0:T(8,128)(2,1)S(1)} %get-tuple-element.16), channel_id=1, source_target_pairs={{0,384},{32,416},{64,448},{96,480},{128,0},{160,32},{192,64},{224,... | collective-permute-start | bytes 393224 | tf_op jit(solution)/shard_map/ppermute | solution.py:264
  163.5 3.1 %collective-permute-start.8 = (bf16[2,256,128]{2,1,0:T(8,128)(2,1)S(1)}, bf16[2,256,128]{2,1,0:T(8,128)(2,1)S(1)}, u32[]{:S(2)}, u32[]{:S(2)}) collective-permute-start(bf16[2,256,128]{2,1,0:T(8,128)(2,1)S(1)} %get-tuple-element.15), channel_id=1, source_target_pairs={{0,256},{32,288},{64,320},{96,352},{128,384},{160,416},{192,448},{... | collective-permute-start | bytes 393224 | tf_op jit(solution)/shard_map/ppermute | solution.py:264
  166.7 1.5 collective-permute-done.7
  168.2 3.7 %collective-permute-done.8 = bf16[2,256,128]{2,1,0:T(8,128)(2,1)S(1)} collective-permute-done((bf16[2,256,128]{2,1,0:T(8,128)(2,1)S(1)}, bf16[2,256,128]{2,1,0:T(8,128)(2,1)S(1)}, u32[]{:S(2)}, u32[]{:S(2)}) %collective-permute-start.8) | collective-permute-done | bytes 131104 | tf_op jit(solution)/shard_map/ppermute | solution.py:264
  171.9 6.6 %collective-permute-start.9 = (bf16[256,128]{1,0:T(8,128)(2,1)S(1)}, bf16[256,128]{1,0:T(8,128)(2,1)S(1)}, u32[]{:S(2)}, u32[]{:S(2)}) collective-permute-start(bf16[256,128]{1,0:T(8,128)(2,1)S(1)} %fusion.7), channel_id=1, source_target_pairs={{0,64},{32,96},{64,0},{96,32},{128,192},{160,224},{192,128},{224,1... | collective-permute-start | bytes 196616 | tf_op jit(solution)/shard_map/ppermute | solution.py:260
  178.6 17.3 %all-to-all-done.1 = bf16[32,128,128]{2,1,0:T(8,128)(2,1)S(1)} async-done(((bf16[32,128,128]{2,1,0:T(8,128)(2,1)}), bf16[32,128,128]{2,1,0:T(8,128)(2,1)S(1)}, u32[]{:S(2)}, u32[]{:S(2)}) %all-to-all-start.1) | async-done | bytes 1048608 | tf_op jit(solution)/shard_map/all_to_all | solution.py:256
  196.5 1.3 copy.22
  (26 shorter events, 1.9 us)
Async XLA Ops:
  0.6 17.7 %copy-start = (f32[256,128]{1,0:T(8,128)S(1)}, f32[256,128]{1,0:T(8,128)}, u32[]{:S(2)}) copy-start(f32[256,128]{1,0:T(8,128)} %param.12) | copy-start | bytes 393220
  3.1 72.6 %all-to-all-start = ((bf16[32,128,128]{2,1,0:T(8,128)(2,1)}), bf16[32,128,128]{2,1,0:T(8,128)(2,1)S(1)}, u32[]{:S(2)}, u32[]{:S(2)}) async-start(bf16[32,128,128]{2,1,0:T(8,128)(2,1)} %shard_map.104), calls=%async_computation | async-start | bytes 2097152 | tf_op jit(solution)/shard_map/all_to_all | solution.py:256
  18.4 16.1 %collective-permute-start = (bf16[256,128]{1,0:T(8,128)(2,1)S(1)}, bf16[256,128]{1,0:T(8,128)(2,1)S(1)}, u32[]{:S(2)}, u32[]{:S(2)}) collective-permute-start(bf16[256,128]{1,0:T(8,128)(2,1)S(1)} %convert_element_type.48), channel_id=1, source_target_pairs={{0,64},{32,96},{64,0},{96,32},{128,192},{160,224},{192,128},{224,1... | collective-permute-start | bytes 196616 | tf_op jit(solution)/shard_map/ppermute | solution.py:260
  75.7 37.7 %copy-start.2 = (bf16[32,128,128]{2,1,0:T(8,128)(2,1)}, bf16[32,128,128]{2,1,0:T(8,128)(2,1)S(1)}, u32[]{:S(2)}) copy-start(bf16[32,128,128]{2,1,0:T(8,128)(2,1)S(1)} %all-to-all-done.x) | copy-start | bytes 3145732
  75.7 58.3 %all-to-all-start.2 = ((bf16[32,128,128]{2,1,0:T(8,128)(2,1)}), bf16[32,128,128]{2,1,0:T(8,128)(2,1)S(1)}, u32[]{:S(2)}, u32[]{:S(2)}) async-start(bf16[32,128,128]{2,1,0:T(8,128)(2,1)} %shard_map.105), calls=%async_computation.2 | async-start | bytes 2097152 | tf_op jit(solution)/shard_map/all_to_all | solution.py:256
  83.5 3.2 %collective-permute-start.1 = (bf16[2,256,128]{2,1,0:T(8,128)(2,1)S(1)}, bf16[2,256,128]{2,1,0:T(8,128)(2,1)S(1)}, u32[]{:S(2)}, u32[]{:S(2)}) collective-permute-start(bf16[2,256,128]{2,1,0:T(8,128)(2,1)S(1)} %maximum_select_fusion.2), channel_id=1, source_target_pairs={{0,32},{32,0},{64,96},{96,64},{128,160},{160,128},{192,224},{224,1... | collective-permute-start | bytes 393224 | tf_op jit(solution)/shard_map/ppermute | solution.py:260
  86.8 10.3 %collective-permute-start.2 = (bf16[2,2,256,128]{3,2,0,1:T(8,128)(2,1)S(1)}, bf16[2,2,256,128]{3,2,0,1:T(8,128)(2,1)S(1)}, u32[]{:S(2)}, u32[]{:S(2)}) collective-permute-start(bf16[2,2,256,128]{3,2,0,1:T(8,128)(2,1)S(1)} %get-tuple-element.17), channel_id=1, source_target_pairs={{0,128},{32,160},{64,192},{96,224},{128,256},{160,288},{192,320},{... | collective-permute-start | bytes 786440 | tf_op jit(solution)/shard_map/ppermute | solution.py:264
  89.0 16.9 %collective-permute-start.3 = (bf16[2,2,256,128]{3,2,0,1:T(8,128)(2,1)S(1)}, bf16[2,2,256,128]{3,2,0,1:T(8,128)(2,1)S(1)}, u32[]{:S(2)}, u32[]{:S(2)}) collective-permute-start(bf16[2,2,256,128]{3,2,0,1:T(8,128)(2,1)S(1)} %get-tuple-element.17), channel_id=1, source_target_pairs={{0,384},{32,416},{64,448},{96,480},{128,0},{160,32},{192,64},{224,... | collective-permute-start | bytes 786440 | tf_op jit(solution)/shard_map/ppermute | solution.py:264
  92.7 13.2 %collective-permute-start.4 = (bf16[2,2,256,128]{3,2,0,1:T(8,128)(2,1)S(1)}, bf16[2,2,256,128]{3,2,0,1:T(8,128)(2,1)S(1)}, u32[]{:S(2)}, u32[]{:S(2)}) collective-permute-start(bf16[2,2,256,128]{3,2,0,1:T(8,128)(2,1)S(1)} %get-tuple-element.17), channel_id=1, source_target_pairs={{0,256},{32,288},{64,320},{96,352},{128,384},{160,416},{192,448},{... | collective-permute-start | bytes 786440 | tf_op jit(solution)/shard_map/ppermute | solution.py:264
  106.0 1.0 copy-start.3
  134.0 5.6 %copy-start.1 = (bf16[32,128,128]{2,1,0:T(8,128)(2,1)}, bf16[32,128,128]{2,1,0:T(8,128)(2,1)S(1)}, u32[]{:S(2)}) copy-start(bf16[32,128,128]{2,1,0:T(8,128)(2,1)S(1)} %all-to-all-done.2.x) | copy-start | bytes 3145732
  134.0 61.8 %all-to-all-start.1 = ((bf16[32,128,128]{2,1,0:T(8,128)(2,1)}), bf16[32,128,128]{2,1,0:T(8,128)(2,1)S(1)}, u32[]{:S(2)}, u32[]{:S(2)}) async-start(bf16[32,128,128]{2,1,0:T(8,128)(2,1)} %get-tuple-element.9), calls=%async_computation.1 | async-start | bytes 2097152 | tf_op jit(solution)/shard_map/all_to_all | solution.py:256
  152.4 3.8 %collective-permute-start.5 = (bf16[4,2,256,128]{3,2,1,0:T(8,128)(2,1)S(1)}, bf16[4,2,256,128]{3,2,1,0:T(8,128)(2,1)S(1)}, u32[]{:S(2)}, u32[]{:S(2)}) collective-permute-start(bf16[4,2,256,128]{3,2,1,0:T(8,128)(2,1)S(1)} %fusion), channel_id=1, source_target_pairs={{0,32},{32,0},{64,96},{96,64},{128,160},{160,128},{192,224},{224,1... | collective-permute-start | bytes 1572872 | tf_op jit(solution)/shard_map/ppermute | solution.py:260
  157.6 9.0 %collective-permute-start.6 = (bf16[2,256,128]{2,1,0:T(8,128)(2,1)S(1)}, bf16[2,256,128]{2,1,0:T(8,128)(2,1)S(1)}, u32[]{:S(2)}, u32[]{:S(2)}) collective-permute-start(bf16[2,256,128]{2,1,0:T(8,128)(2,1)S(1)} %get-tuple-element.14), channel_id=1, source_target_pairs={{0,128},{32,160},{64,192},{96,224},{128,256},{160,288},{192,320},{... | collective-permute-start | bytes 393224 | tf_op jit(solution)/shard_map/ppermute | solution.py:264
  159.8 8.4 %collective-permute-start.7 = (bf16[2,256,128]{2,1,0:T(8,128)(2,1)S(1)}, bf16[2,256,128]{2,1,0:T(8,128)(2,1)S(1)}, u32[]{:S(2)}, u32[]{:S(2)}) collective-permute-start(bf16[2,256,128]{2,1,0:T(8,128)(2,1)S(1)} %get-tuple-element.16), channel_id=1, source_target_pairs={{0,384},{32,416},{64,448},{96,480},{128,0},{160,32},{192,64},{224,... | collective-permute-start | bytes 393224 | tf_op jit(solution)/shard_map/ppermute | solution.py:264
  163.5 8.4 %collective-permute-start.8 = (bf16[2,256,128]{2,1,0:T(8,128)(2,1)S(1)}, bf16[2,256,128]{2,1,0:T(8,128)(2,1)S(1)}, u32[]{:S(2)}, u32[]{:S(2)}) collective-permute-start(bf16[2,256,128]{2,1,0:T(8,128)(2,1)S(1)} %get-tuple-element.15), channel_id=1, source_target_pairs={{0,256},{32,288},{64,320},{96,352},{128,384},{160,416},{192,448},{... | collective-permute-start | bytes 393224 | tf_op jit(solution)/shard_map/ppermute | solution.py:264
  171.9 25.9 %collective-permute-start.9 = (bf16[256,128]{1,0:T(8,128)(2,1)S(1)}, bf16[256,128]{1,0:T(8,128)(2,1)S(1)}, u32[]{:S(2)}, u32[]{:S(2)}) collective-permute-start(bf16[256,128]{1,0:T(8,128)(2,1)S(1)} %fusion.7), channel_id=1, source_target_pairs={{0,64},{32,96},{64,0},{96,32},{128,192},{160,224},{192,128},{224,1... | collective-permute-start | bytes 196616 | tf_op jit(solution)/shard_map/ppermute | solution.py:260

commit v4 on v3

--- a/solution.py
+++ b/solution.py
@@ -260,10 +260,6 @@
     return lax.ppermute(value, "dp", [(i, i ^ bit) for i in range(16)])
 
 
-def turn(value, by):
-    return lax.ppermute(value, "dp", [(i, (i + 4 * by) % 16) for i in range(16)])
-
-
 def place():
     index = lax.axis_index("dp")
     return index // 4, index // 2 % 2, index % 2
@@ -280,7 +276,7 @@
     whole = jnp.zeros((4,) + both.shape, both.dtype)
     whole = lax.dynamic_update_index_in_dim(whole, both, y, 0)
     for by in (1, 3, 2):
-        whole = lax.dynamic_update_index_in_dim(whole, turn(both, by), (y - by) % 4, 0)
+        whole = lax.dynamic_update_index_in_dim(whole, swap(both, 4 * by), y ^ by, 0)
     return whole.reshape(coarse, fine, fine)
 
 
@@ -291,8 +287,8 @@
     kept = lax.dynamic_index_in_dim(parts, core, 2, keepdims=False) + swap(away.astype(bf16), 1).astype(f32)
     total = lax.dynamic_index_in_dim(kept, y, 0, keepdims=False)
     for by in (1, 3, 2):
-        away = lax.dynamic_index_in_dim(kept, (y + by) % 4, 0, keepdims=False)
-        total = total + turn(away.astype(bf16), by).astype(f32)
+        away = lax.dynamic_index_in_dim(kept, y ^ by, 0, keepdims=False)
+        total = total + swap(away.astype(bf16), 4 * by).astype(f32)
     away = lax.dynamic_index_in_dim(total, 1 - z_hi, 0, keepdims=False)
     return lax.dynamic_index_in_dim(total, z_hi, 0, keepdims=False) + swap(away.astype(bf16), 2).astype(f32)
 

time: 199 us -> 199 us (level)
    ppermute x4 -> x10, starting transfers between devices: 18.7 us -> 38.3 us  [swap(): return lax.ppermute(value, 'dp', [(i, i ^ bit) for i in range(16)])]
    ppermute x6 -> x0, starting transfers between devices: 18 us -> none  [turn(): lax.ppermute(value, 'dp', [(i, (i + 4 * by) % 16) for i in range(16)])]
    ppermute x6 -> x0, waiting for transfers between devices: 14.9 us -> none  [turn(): lax.ppermute(value, 'dp', [(i, (i + 4 * by) % 16) for i in range(16)])]
    ppermute x4 -> x10, waiting for transfers between devices: 8.71 us -> 22.2 us  [swap(): return lax.ppermute(value, 'dp', [(i, i ^ bit) for i in range(16)])]
where the time goes in v4:
time: 199 us
  waiting for transfers between devices  89.5 us (45%)
  starting transfers between devices  66.9 us (34%)
  Pallas kernels  34.2 us (17%)
  local copies, waits for them, and re-layouts  4.72 us (2%)
  other arithmetic  2.14 us (1%)
    all_to_all x3, waiting for transfers between devices, to_owners(): return lax.all_to_all(blocks, 'ctx', 0, 0, tiled=True)  67.3 us
    ppermute x10, starting transfers between devices, swap(): return lax.ppermute(value, 'dp', [(i, i ^ bit) for i in range(16)])  38.3 us
    pallas_call x3, Pallas kernels, call(): pl.pallas_call(kernel, out_shape=out_shape, in_specs=[anywhere] * len(arg...  29.5 us
    all_to_all x3, starting transfers between devices, to_owners(): return lax.all_to_all(blocks, 'ctx', 0, 0, tiled=True)  28.6 us
    ppermute x10, waiting for transfers between devices, swap(): return lax.ppermute(value, 'dp', [(i, i ^ bit) for i in range(16)])  22.2 us
    pallas_call x2, Pallas kernels, to_blocks(): pl.pallas_call(kernel, grid=(coarse // blocks_a_step,), in_specs=[wide] *...  4.68 us
  transfers between devices with their start and end apart: 13, of which 10 were waited for; matrix products, arithmetic and copies ran while one was open for 3% of the time, Pallas kernels for 16%

profile of v4, /device:TPU:56, one launch (start us, length us, event | category | flops | bytes accessed | tf_op | source)
XLA Modules:
  0.0 198.5 jit_solution(14987358457543078866)
XLA Ops:
  0.6 2.5 %shard_map.104 = bf16[32,128,128]{2,1,0:T(8,128)(2,1)} custom-call(bf16[1,128,4096]{2,1,0:T(8,128)(2,1)} %grad_ref.1, bf16[1,128,4096]{2,1,0:T(8,128)(2,1)} %query_ref.1), custom_call_target="tpu_custom_call" | custom-call | tf_op jit(solution)/shard_map/pallas_call | solution.py:241
  3.1 15.2 %all-to-all-start = ((bf16[32,128,128]{2,1,0:T(8,128)(2,1)}), bf16[32,128,128]{2,1,0:T(8,128)(2,1)S(1)}, u32[]{:S(2)}, u32[]{:S(2)}) async-start(bf16[32,128,128]{2,1,0:T(8,128)(2,1)} %shard_map.104), calls=%async_computation | async-start | bytes 2097152 | tf_op jit(solution)/shard_map/all_to_all | solution.py:256
  18.4 8.2 %collective-permute-start = (bf16[256,128]{1,0:T(8,128)(2,1)S(1)}, bf16[256,128]{1,0:T(8,128)(2,1)S(1)}, u32[]{:S(2)}, u32[]{:S(2)}) collective-permute-start(bf16[256,128]{1,0:T(8,128)(2,1)S(1)} %convert_element_type.48), channel_id=1, source_target_pairs={{0,64},{32,96},{64,0},{96,32},{128,192},{160,224},{192,128},{224,1... | collective-permute-start | bytes 196616 | tf_op jit(solution)/shard_map/ppermute | solution.py:260
  26.6 2.2 %shard_map.105 = bf16[32,128,128]{2,1,0:T(8,128)(2,1)} custom-call(bf16[1,128,4096]{2,1,0:T(8,128)(2,1)} %value_ref.1), custom_call_target="tpu_custom_call" | custom-call | tf_op jit(solution)/shard_map/pallas_call | solution.py:241
  28.8 5.6 %collective-permute-done = bf16[256,128]{1,0:T(8,128)(2,1)S(1)} collective-permute-done((bf16[256,128]{1,0:T(8,128)(2,1)S(1)}, bf16[256,128]{1,0:T(8,128)(2,1)S(1)}, u32[]{:S(2)}, u32[]{:S(2)}) %collective-permute-start) | collective-permute-done | bytes 65568 | tf_op jit(solution)/shard_map/ppermute | solution.py:260
  34.5 41.2 %all-to-all-done.x = bf16[32,128,128]{2,1,0:T(8,128)(2,1)S(1)} async-done(((bf16[32,128,128]{2,1,0:T(8,128)(2,1)}), bf16[32,128,128]{2,1,0:T(8,128)(2,1)S(1)}, u32[]{:S(2)}, u32[]{:S(2)}) %all-to-all-start) | async-done | bytes 1048608 | tf_op jit(solution)/shard_map/all_to_all | solution.py:256
  75.7 7.7 %all-to-all-start.2 = ((bf16[32,128,128]{2,1,0:T(8,128)(2,1)}), bf16[32,128,128]{2,1,0:T(8,128)(2,1)S(1)}, u32[]{:S(2)}, u32[]{:S(2)}) async-start(bf16[32,128,128]{2,1,0:T(8,128)(2,1)} %shard_map.105), calls=%async_computation.2 | async-start | bytes 2097152 | tf_op jit(solution)/shard_map/all_to_all | solution.py:256
  83.5 1.9 collective-permute-start.1
  85.5 1.3 collective-permute-done.1
  86.8 2.7 %collective-permute-start.2 = (bf16[2,2,256,128]{3,2,0,1:T(8,128)(2,1)S(1)}, bf16[2,2,256,128]{3,2,0,1:T(8,128)(2,1)S(1)}, u32[]{:S(2)}, u32[]{:S(2)}) collective-permute-start(bf16[2,2,256,128]{3,2,0,1:T(8,128)(2,1)S(1)} %get-tuple-element.17), channel_id=1, source_target_pairs={{0,128},{32,160},{64,192},{96,224},{128,0},{160,32},{192,64},{224,... | collective-permute-start | bytes 786440 | tf_op jit(solution)/shard_map/ppermute | solution.py:260
  89.5 3.0 %collective-permute-start.3 = (bf16[2,2,256,128]{3,2,0,1:T(8,128)(2,1)S(1)}, bf16[2,2,256,128]{3,2,0,1:T(8,128)(2,1)S(1)}, u32[]{:S(2)}, u32[]{:S(2)}) collective-permute-start(bf16[2,2,256,128]{3,2,0,1:T(8,128)(2,1)S(1)} %get-tuple-element.17), channel_id=1, source_target_pairs={{0,384},{32,416},{64,448},{96,480},{128,256},{160,288},{192,320},{... | collective-permute-start | bytes 786440 | tf_op jit(solution)/shard_map/ppermute | solution.py:260
  92.4 4.2 %collective-permute-start.4 = (bf16[2,2,256,128]{3,2,0,1:T(8,128)(2,1)S(1)}, bf16[2,2,256,128]{3,2,0,1:T(8,128)(2,1)S(1)}, u32[]{:S(2)}, u32[]{:S(2)}) collective-permute-start(bf16[2,2,256,128]{3,2,0,1:T(8,128)(2,1)S(1)} %get-tuple-element.17), channel_id=1, source_target_pairs={{0,256},{32,288},{64,320},{96,352},{128,384},{160,416},{192,448},{... | collective-permute-start | bytes 786440 | tf_op jit(solution)/shard_map/ppermute | solution.py:260
  97.1 9.2 %collective-permute-done.3 = bf16[2,2,256,128]{3,2,0,1:T(8,128)(2,1)S(1)} collective-permute-done((bf16[2,2,256,128]{3,2,0,1:T(8,128)(2,1)S(1)}, bf16[2,2,256,128]{3,2,0,1:T(8,128)(2,1)S(1)}, u32[]{:S(2)}, u32[]{:S(2)}) %collective-permute-start.3) | collective-permute-done | bytes 262176 | tf_op jit(solution)/shard_map/ppermute | solution.py:260
  106.4 1.0 copy-done.3
  107.4 6.4 %shard_map.106.taps = f32[16,256,256]{2,1,0:T(8,128)} custom-call(bf16[32,128,128]{2,1,0:T(8,128)(2,1)} %bitcast.55, bf16[512,768]{1,0:T(8,128)(2,1)} %constant.104.clone.forward, bf16[256,768]{1,0:T(8,128)(2,1)} %constant.107.clone.inner, f32[32,2,128,128]{3,2,1,0:T(8,128)} %constant.106.clone.twiddle), custom_call_target="tpu_custom_call" | custom-call | flops 3221225472 | bytes 8388608 | tf_op jit(solution)/shard_map/pallas_call | solution.py:214
  113.8 11.6 %shard_map.107 = (bf16[32,128,128]{2,1,0:T(8,128)(2,1)}, f32[16,256,256]{2,1,0:T(8,128)}) custom-call(bf16[32,128,128]{2,1,0:T(8,128)(2,1)} %copy-done.2, bf16[512,768]{1,0:T(8,128)(2,1)} %constant.104.clone.forward, bf16[256,768]{1,0:T(8,128)(2,1)} %constant.107.clone.inner, f32[32,2,128,128]{3,2,1,0:T(8,128)} %constant.106.clone.twiddle, ...), custom_call_target="tpu_custom_call" | custom-call | flops 6442450944 | bytes 8388608 | tf_op jit(solution)/shard_map/pallas_call | solution.py:214
  125.5 8.6 %all-to-all-done.2.x = bf16[32,128,128]{2,1,0:T(8,128)(2,1)S(1)} async-done(((bf16[32,128,128]{2,1,0:T(8,128)(2,1)}), bf16[32,128,128]{2,1,0:T(8,128)(2,1)S(1)}, u32[]{:S(2)}, u32[]{:S(2)}) %all-to-all-start.2) | async-done | bytes 1048608 | tf_op jit(solution)/shard_map/all_to_all | solution.py:256
  134.0 5.6 %all-to-all-start.1 = ((bf16[32,128,128]{2,1,0:T(8,128)(2,1)}), bf16[32,128,128]{2,1,0:T(8,128)(2,1)S(1)}, u32[]{:S(2)}, u32[]{:S(2)}) async-start(bf16[32,128,128]{2,1,0:T(8,128)(2,1)} %get-tuple-element.9), calls=%async_computation.1 | async-start | bytes 2097152 | tf_op jit(solution)/shard_map/all_to_all | solution.py:256
  139.7 11.4 %shard_map.108 = f32[32,128,128]{2,1,0:T(8,128)} custom-call(bf16[32,128,128]{2,1,0:T(8,128)(2,1)} %copy-done.1, bf16[512,768]{1,0:T(8,128)(2,1)} %constant.104.clone.forward, bf16[256,768]{1,0:T(8,128)(2,1)} %constant.107.clone.inner, f32[32,2,128,128]{3,2,1,0:T(8,128)} %constant.106.clone.twiddle, f32[16,256,256]{2,1,0:T(8,128)} %get-tuple-element.11.prod, ...), custom_call_target="tpu_custom_call" | custom-call | flops 6442450944 | bytes 8388608 | tf_op jit(solution)/shard_map/pallas_call | solution.py:214
  151.1 1.3 fusion
  152.4 1.9 collective-permute-start.5
  154.4 1.9 collective-permute-done.5
  156.2 1.3 bitcast_add_fusion
  157.6 2.7 %collective-permute-start.6 = (bf16[2,256,128]{2,1,0:T(8,128)(2,1)S(1)}, bf16[2,256,128]{2,1,0:T(8,128)(2,1)S(1)}, u32[]{:S(2)}, u32[]{:S(2)}) collective-permute-start(bf16[2,256,128]{2,1,0:T(8,128)(2,1)S(1)} %get-tuple-element.14), channel_id=1, source_target_pairs={{0,128},{32,160},{64,192},{96,224},{128,0},{160,32},{192,64},{224,... | collective-permute-start | bytes 393224 | tf_op jit(solution)/shard_map/ppermute | solution.py:260
  160.3 3.0 %collective-permute-start.7 = (bf16[2,256,128]{2,1,0:T(8,128)(2,1)S(1)}, bf16[2,256,128]{2,1,0:T(8,128)(2,1)S(1)}, u32[]{:S(2)}, u32[]{:S(2)}) collective-permute-start(bf16[2,256,128]{2,1,0:T(8,128)(2,1)S(1)} %get-tuple-element.16), channel_id=1, source_target_pairs={{0,384},{32,416},{64,448},{96,480},{128,256},{160,288},{192,320},{... | collective-permute-start | bytes 393224 | tf_op jit(solution)/shard_map/ppermute | solution.py:260
  163.3 4.2 %collective-permute-start.8 = (bf16[2,256,128]{2,1,0:T(8,128)(2,1)S(1)}, bf16[2,256,128]{2,1,0:T(8,128)(2,1)S(1)}, u32[]{:S(2)}, u32[]{:S(2)}) collective-permute-start(bf16[2,256,128]{2,1,0:T(8,128)(2,1)S(1)} %get-tuple-element.15), channel_id=1, source_target_pairs={{0,256},{32,288},{64,320},{96,352},{128,384},{160,416},{192,448},{... | collective-permute-start | bytes 393224 | tf_op jit(solution)/shard_map/ppermute | solution.py:260
  167.5 1.2 collective-permute-done.7
  168.7 3.0 %collective-permute-done.8 = bf16[2,256,128]{2,1,0:T(8,128)(2,1)S(1)} collective-permute-done((bf16[2,256,128]{2,1,0:T(8,128)(2,1)S(1)}, bf16[2,256,128]{2,1,0:T(8,128)(2,1)S(1)}, u32[]{:S(2)}, u32[]{:S(2)}) %collective-permute-start.8) | collective-permute-done | bytes 131104 | tf_op jit(solution)/shard_map/ppermute | solution.py:260
  171.7 6.6 %collective-permute-start.9 = (bf16[256,128]{1,0:T(8,128)(2,1)S(1)}, bf16[256,128]{1,0:T(8,128)(2,1)S(1)}, u32[]{:S(2)}, u32[]{:S(2)}) collective-permute-start(bf16[256,128]{1,0:T(8,128)(2,1)S(1)} %fusion.7), channel_id=1, source_target_pairs={{0,64},{32,96},{64,0},{96,32},{128,192},{160,224},{192,128},{224,1... | collective-permute-start | bytes 196616 | tf_op jit(solution)/shard_map/ppermute | solution.py:260
  178.3 17.5 %all-to-all-done.1 = bf16[32,128,128]{2,1,0:T(8,128)(2,1)S(1)} async-done(((bf16[32,128,128]{2,1,0:T(8,128)(2,1)}), bf16[32,128,128]{2,1,0:T(8,128)(2,1)S(1)}, u32[]{:S(2)}, u32[]{:S(2)}) %all-to-all-start.1) | async-done | bytes 1048608 | tf_op jit(solution)/shard_map/all_to_all | solution.py:256
  196.5 1.3 copy.22
  197.8 0.7 fusion.6
  (26 shorter events, 1.4 us)
Async XLA Ops:
  0.6 17.7 %copy-start = (f32[256,128]{1,0:T(8,128)S(1)}, f32[256,128]{1,0:T(8,128)}, u32[]{:S(2)}) copy-start(f32[256,128]{1,0:T(8,128)} %param.12) | copy-start | bytes 393220
  3.1 72.6 %all-to-all-start = ((bf16[32,128,128]{2,1,0:T(8,128)(2,1)}), bf16[32,128,128]{2,1,0:T(8,128)(2,1)S(1)}, u32[]{:S(2)}, u32[]{:S(2)}) async-start(bf16[32,128,128]{2,1,0:T(8,128)(2,1)} %shard_map.104), calls=%async_computation | async-start | bytes 2097152 | tf_op jit(solution)/shard_map/all_to_all | solution.py:256
  18.4 16.1 %collective-permute-start = (bf16[256,128]{1,0:T(8,128)(2,1)S(1)}, bf16[256,128]{1,0:T(8,128)(2,1)S(1)}, u32[]{:S(2)}, u32[]{:S(2)}) collective-permute-start(bf16[256,128]{1,0:T(8,128)(2,1)S(1)} %convert_element_type.48), channel_id=1, source_target_pairs={{0,64},{32,96},{64,0},{96,32},{128,192},{160,224},{192,128},{224,1... | collective-permute-start | bytes 196616 | tf_op jit(solution)/shard_map/ppermute | solution.py:260
  75.7 38.1 %copy-start.2 = (bf16[32,128,128]{2,1,0:T(8,128)(2,1)}, bf16[32,128,128]{2,1,0:T(8,128)(2,1)S(1)}, u32[]{:S(2)}) copy-start(bf16[32,128,128]{2,1,0:T(8,128)(2,1)S(1)} %all-to-all-done.x) | copy-start | bytes 3145732
  75.7 58.3 %all-to-all-start.2 = ((bf16[32,128,128]{2,1,0:T(8,128)(2,1)}), bf16[32,128,128]{2,1,0:T(8,128)(2,1)S(1)}, u32[]{:S(2)}, u32[]{:S(2)}) async-start(bf16[32,128,128]{2,1,0:T(8,128)(2,1)} %shard_map.105), calls=%async_computation.2 | async-start | bytes 2097152 | tf_op jit(solution)/shard_map/all_to_all | solution.py:256
  83.5 3.2 %collective-permute-start.1 = (bf16[2,256,128]{2,1,0:T(8,128)(2,1)S(1)}, bf16[2,256,128]{2,1,0:T(8,128)(2,1)S(1)}, u32[]{:S(2)}, u32[]{:S(2)}) collective-permute-start(bf16[2,256,128]{2,1,0:T(8,128)(2,1)S(1)} %maximum_select_fusion.2), channel_id=1, source_target_pairs={{0,32},{32,0},{64,96},{96,64},{128,160},{160,128},{192,224},{224,1... | collective-permute-start | bytes 393224 | tf_op jit(solution)/shard_map/ppermute | solution.py:260
  86.8 10.3 %collective-permute-start.2 = (bf16[2,2,256,128]{3,2,0,1:T(8,128)(2,1)S(1)}, bf16[2,2,256,128]{3,2,0,1:T(8,128)(2,1)S(1)}, u32[]{:S(2)}, u32[]{:S(2)}) collective-permute-start(bf16[2,2,256,128]{3,2,0,1:T(8,128)(2,1)S(1)} %get-tuple-element.17), channel_id=1, source_target_pairs={{0,128},{32,160},{64,192},{96,224},{128,0},{160,32},{192,64},{224,... | collective-permute-start | bytes 786440 | tf_op jit(solution)/shard_map/ppermute | solution.py:260
  89.5 16.8 %collective-permute-start.3 = (bf16[2,2,256,128]{3,2,0,1:T(8,128)(2,1)S(1)}, bf16[2,2,256,128]{3,2,0,1:T(8,128)(2,1)S(1)}, u32[]{:S(2)}, u32[]{:S(2)}) collective-permute-start(bf16[2,2,256,128]{3,2,0,1:T(8,128)(2,1)S(1)} %get-tuple-element.17), channel_id=1, source_target_pairs={{0,384},{32,416},{64,448},{96,480},{128,256},{160,288},{192,320},{... | collective-permute-start | bytes 786440 | tf_op jit(solution)/shard_map/ppermute | solution.py:260
  92.4 13.9 %collective-permute-start.4 = (bf16[2,2,256,128]{3,2,0,1:T(8,128)(2,1)S(1)}, bf16[2,2,256,128]{3,2,0,1:T(8,128)(2,1)S(1)}, u32[]{:S(2)}, u32[]{:S(2)}) collective-permute-start(bf16[2,2,256,128]{3,2,0,1:T(8,128)(2,1)S(1)} %get-tuple-element.17), channel_id=1, source_target_pairs={{0,256},{32,288},{64,320},{96,352},{128,384},{160,416},{192,448},{... | collective-permute-start | bytes 786440 | tf_op jit(solution)/shard_map/ppermute | solution.py:260
  106.4 1.0 copy-start.3
  134.0 5.6 %copy-start.1 = (bf16[32,128,128]{2,1,0:T(8,128)(2,1)}, bf16[32,128,128]{2,1,0:T(8,128)(2,1)S(1)}, u32[]{:S(2)}) copy-start(bf16[32,128,128]{2,1,0:T(8,128)(2,1)S(1)} %all-to-all-done.2.x) | copy-start | bytes 3145732
  134.0 61.8 %all-to-all-start.1 = ((bf16[32,128,128]{2,1,0:T(8,128)(2,1)}), bf16[32,128,128]{2,1,0:T(8,128)(2,1)S(1)}, u32[]{:S(2)}, u32[]{:S(2)}) async-start(bf16[32,128,128]{2,1,0:T(8,128)(2,1)} %get-tuple-element.9), calls=%async_computation.1 | async-start | bytes 2097152 | tf_op jit(solution)/shard_map/all_to_all | solution.py:256
  152.4 3.8 %collective-permute-start.5 = (bf16[4,2,256,128]{3,2,1,0:T(8,128)(2,1)S(1)}, bf16[4,2,256,128]{3,2,1,0:T(8,128)(2,1)S(1)}, u32[]{:S(2)}, u32[]{:S(2)}) collective-permute-start(bf16[4,2,256,128]{3,2,1,0:T(8,128)(2,1)S(1)} %fusion), channel_id=1, source_target_pairs={{0,32},{32,0},{64,96},{96,64},{128,160},{160,128},{192,224},{224,1... | collective-permute-start | bytes 1572872 | tf_op jit(solution)/shard_map/ppermute | solution.py:260
  157.6 9.9 %collective-permute-start.6 = (bf16[2,256,128]{2,1,0:T(8,128)(2,1)S(1)}, bf16[2,256,128]{2,1,0:T(8,128)(2,1)S(1)}, u32[]{:S(2)}, u32[]{:S(2)}) collective-permute-start(bf16[2,256,128]{2,1,0:T(8,128)(2,1)S(1)} %get-tuple-element.14), channel_id=1, source_target_pairs={{0,128},{32,160},{64,192},{96,224},{128,0},{160,32},{192,64},{224,... | collective-permute-start | bytes 393224 | tf_op jit(solution)/shard_map/ppermute | solution.py:260
  160.3 8.4 %collective-permute-start.7 = (bf16[2,256,128]{2,1,0:T(8,128)(2,1)S(1)}, bf16[2,256,128]{2,1,0:T(8,128)(2,1)S(1)}, u32[]{:S(2)}, u32[]{:S(2)}) collective-permute-start(bf16[2,256,128]{2,1,0:T(8,128)(2,1)S(1)} %get-tuple-element.16), channel_id=1, source_target_pairs={{0,384},{32,416},{64,448},{96,480},{128,256},{160,288},{192,320},{... | collective-permute-start | bytes 393224 | tf_op jit(solution)/shard_map/ppermute | solution.py:260
  163.3 8.4 %collective-permute-start.8 = (bf16[2,256,128]{2,1,0:T(8,128)(2,1)S(1)}, bf16[2,256,128]{2,1,0:T(8,128)(2,1)S(1)}, u32[]{:S(2)}, u32[]{:S(2)}) collective-permute-start(bf16[2,256,128]{2,1,0:T(8,128)(2,1)S(1)} %get-tuple-element.15), channel_id=1, source_target_pairs={{0,256},{32,288},{64,320},{96,352},{128,384},{160,416},{192,448},{... | collective-permute-start | bytes 393224 | tf_op jit(solution)/shard_map/ppermute | solution.py:260
  171.7 26.1 %collective-permute-start.9 = (bf16[256,128]{1,0:T(8,128)(2,1)S(1)}, bf16[256,128]{1,0:T(8,128)(2,1)S(1)}, u32[]{:S(2)}, u32[]{:S(2)}) collective-permute-start(bf16[256,128]{1,0:T(8,128)(2,1)S(1)} %fusion.7), channel_id=1, source_target_pairs={{0,64},{32,96},{64,0},{96,32},{128,192},{160,224},{192,128},{224,1... | collective-permute-start | bytes 196616 | tf_op jit(solution)/shard_map/ppermute | solution.py:260
